TPU v7x, 32 devices: a whole 2x2x4 slice. The times are simulated.
32 devices in a mesh: phase: 4 (over x, core), seq: 8 (over z, y).
Axes of the slice: x: 2, y: 2, z: 4, core: 2. Of those that a mesh axis runs over, the one named last changes fastest.
Arguments:
- frames: bfloat16 [4, 1280, 1024], P('phase', 'seq'), may hold values from -6 to 6
- lengths: int32 [4, 8], P('phase'), may hold values from 1 to 640, 1280 in all within a row
- w_query: bfloat16 [4, 1024, 1024], P('phase', None, 'seq'), may hold values from -1 to 1
- w_key: bfloat16 [4, 1024, 1024], P('phase', None, 'seq'), may hold values from -1 to 1
- w_value: bfloat16 [4, 1024, 1024], P('phase', None, 'seq'), may hold values from -0.1875 to 0.1875
- w_output: bfloat16 [4, 1024, 1024], P('phase', None, 'seq'), may hold values from -0.1875 to 0.1875
- conv_in: bfloat16 [4, 1024, 2048], P('phase', None, 'seq'), may hold values from -0.1875 to 0.1875
- conv_taps: bfloat16 [4, 31, 1024], P('phase'), may hold values from -1 to 1
- conv_out: bfloat16 [4, 1024, 1024], P('phase', None, 'seq'), may hold values from -0.1875 to 0.1875
Outputs:
- handed: bfloat16 [4, 1280, 1024], P('phase', 'seq')
Inputs may be any that keep to these rules, and one draw needn't show every extreme that they name: Each phase's lengths sum to 1280 and the largest equals 640.
All inputs are finite; a program needn't handle non-finite values.
Results may differ from a plain program's by a relative error of at most 0.0085.
Values may be sent and summed in bfloat16 or wider, within the bound.
A program may use at most 64 MiB of HBM per device.

v0:
```python
import functools
import math

import jax
import jax.numpy as jnp
from jax import lax
from jax.experimental import pallas as pl
from jax.experimental.pallas import tpu as pltpu
from jax.sharding import PartitionSpec as P

HEADS = 16
KERNEL = 31
MESH = pl.DeviceIdType.MESH


def padded_2(block, sides, width):
    for axis, dim in sides:
        count = lax.axis_size(axis)
        forward = [(i, i + 1) for i in range(count - 1)]
        backward = [(target, source) for source, target in forward]
        low = lax.ppermute(
            lax.slice_in_dim(block, block.shape[dim] - width, None, axis=dim), axis, forward
        )
        high = lax.ppermute(lax.slice_in_dim(block, 0, width, axis=dim), axis, backward)
        block = jnp.concatenate([low, block, high], axis=dim)
    return block


def passed_along(block, axis, distance):
    devices = range(lax.axis_size(axis))
    route = [((i - distance) % len(devices), i) for i in devices]
    return lax.ppermute(block, axis, route)


def layer_norm(values):
    centre = values - jnp.mean(values, axis=-1, keepdims=True)
    spread = jnp.mean(centre * centre, axis=-1, keepdims=True)
    return centre * lax.rsqrt(spread + 1e-05)


def segment_ids(positions, lengths):
    order = jnp.arange(lengths.shape[0], dtype=jnp.int32)
    bounds = jnp.sum(jnp.where(order[None, :] <= order[:, None], lengths[None, :], 0), axis=1)
    return jnp.sum((positions[:, None] >= bounds[None, :]).astype(jnp.int32), axis=1)


def ring_index(place, shards):
    place = lax.rem(place + shards, shards)
    late = lax.div(place, shards // 2)
    return (1 - late) * (2 * place) + late * (2 * (shards - 1 - place) + 1)


def block_kernel(
    shards,
    head_size,
    frames_ref,
    seg_row_ref,
    seg_col_ref,
    near_ref,
    taps_ref,
    query_ref,
    key_ref,
    value_ref,
    w_a_ref,
    w_b_ref,
    w_c_ref,
    handed_ref,
    hidden,
    qkv,
    full_a_ref,
    full_b_ref,
    full_c_ref,
    attended_ref,
    after,
    gates,
    edge,
    padded,
    depthwise,
    leaving,
    normed,
    query,
    keys,
    values,
    outbox,
    send_sem,
    recv_sem,
    own_sem,
    out_send,
    out_recv,
    in_sem,
    edge_send,
    edge_recv,
    leave_send,
    leave_recv,
):
    rows = frames_ref.shape[0]
    depth = frames_ref.shape[1]
    width = query_ref.shape[1]
    loads_in = [pltpu.make_async_copy(frames_ref, hidden, in_sem.at[3])]
    for i, ref in enumerate((query_ref, key_ref, value_ref)):
        loads_in.append(
            pltpu.make_async_copy(ref, qkv.at[:, pl.ds(i * width, width)], in_sem.at[i])
        )
    for copy in loads_in:
        copy.start()
    steps = shards // 2
    me = lax.axis_index("seq")
    odd = lax.rem(me, 2)
    place = (1 - odd) * lax.div(me, 2) + odd * (shards - 1 - lax.div(me, 2))
    right, left = ring_index(place + 1, shards), ring_index(place - 1, shards)

    barrier = pltpu.get_barrier_semaphore()
    for away in range(1, shards):
        peer = lax.rem(me + away, shards)
        pl.semaphore_signal(barrier, inc=1, device_id={"seq": peer}, device_id_type=MESH)
    phase = lax.axis_index("phase")
    phases = lax.axis_size("phase")
    phase_next = lax.rem(phase + 1, phases)
    phase_back = lax.rem(phase + phases - 1, phases)
    for peer in (phase_next, phase_back):
        pl.semaphore_signal(barrier, inc=1, device_id={"phase": peer}, device_id_type=MESH)

    loads_in[0].wait()
    own_rows = pl.ds(pl.multiple_of(me * rows, rows), rows)
    normed[own_rows, :] = layer_norm(hidden[...].astype(jnp.float32)).astype(jnp.bfloat16)
    pl.semaphore_wait(barrier, shards + 1)

    pairs = ((w_a_ref, full_a_ref), (w_b_ref, full_b_ref), (w_c_ref, full_c_ref))

    def view(load, owner, half):
        if load == 0:
            first, size = (0, rows) if half is None else (half * (rows // 2), rows // 2)
            return normed.at[pl.ds(pl.multiple_of(owner * rows + first, 16), size), :]
        own, full = pairs[load - 1]
        depth = own.shape[0]
        first, size = (0, depth) if half is None else (half * (depth // 2), depth // 2)
        return full.at[owner, pl.ds(first, size), :]

    def hop(load, step, way):
        half = way if step == steps - 1 else None
        owner = ring_index(place - step if way == 0 else place + step, shards)
        target = view(load, owner, half)
        source = target
        if load > 0 and step == 0:
            source = pairs[load - 1][0]
            if half is not None:
                depth = source.shape[0] // 2
                source = source.at[pl.ds(half * depth, depth), :]
        return pltpu.make_async_remote_copy(
            src_ref=source,
            dst_ref=target,
            send_sem=send_sem.at[load, step, way],
            recv_sem=recv_sem.at[load, step, way],
            device_id={"seq": right if way == 0 else left},
            device_id_type=MESH,
        )

    def arrive(load, step):
        for way in range(2):
            hop(load, step, way).wait_recv()

    def send(load, step):
        for way in range(2):
            hop(load, step, way).start()

    def project(owner):
        at = pl.ds(pl.multiple_of(owner * rows, rows), rows)
        block = normed[at, :]
        both = jnp.dot(block, qkv[...], preferred_element_type=jnp.float32).astype(jnp.bfloat16)
        query[at, :] = both[:, :width] * jnp.bfloat16(1.0 / math.sqrt(head_size))
        keys[at, :] = both[:, width : 2 * width]
        values[at, :] = both[:, 2 * width :]

    kept = []
    send(0, 0)
    for load in (1, 2, 3):
        own, full = pairs[load - 1]
        copy = pltpu.make_async_copy(own, full.at[me], own_sem.at[load - 1])
        copy.start()
        kept.append(copy)
    for copy in loads_in[1:]:
        copy.wait()
    project(me)
    for step in range(steps):
        arrive(0, step)
        if step < steps - 1:
            send(0, step + 1)
        if step == steps - 2:
            send(1, 0)
            send(2, 0)
        project(ring_index(place - 1 - step, shards))
        if step < steps - 1:
            project(ring_index(place + 1 + step, shards))

    lane = lax.broadcasted_iota(jnp.int32, (rows, width), 1)
    my_columns = pl.ds(pl.multiple_of(me * width, 128), width)

    def attend(owner):
        at = pl.ds(pl.multiple_of(owner * rows, rows), rows)
        block = query[at, :]
        allowed = seg_row_ref[at, :] == seg_col_ref[...]
        result = jnp.zeros((rows, width), jnp.float32)
        for head in range(width // head_size):
            mine = (lane >= head * head_size) & (lane < (head + 1) * head_size)
            scores = lax.dot_general(
                jnp.where(mine, block, jnp.bfloat16(0)),
                keys[...],
                (((1,), (1,)), ((), ())),
                preferred_element_type=jnp.float32,
            )
            scores = jnp.where(allowed, scores, -1e30)
            peak = jnp.max(scores, axis=1, keepdims=True)
            expw = jnp.exp(scores - peak)
            total = jnp.sum(expw, axis=1, keepdims=True)
            mixed = jnp.dot(
                expw.astype(jnp.bfloat16), values[...], preferred_element_type=jnp.float32
            )
            result = jnp.where(mine, mixed / total, result)
        return result.astype(jnp.bfloat16)

    def out_copy(away):
        peer = lax.rem(me + away, shards)
        return pltpu.make_async_remote_copy(
            src_ref=outbox.at[away - 1],
            dst_ref=attended_ref.at[:, my_columns],
            send_sem=out_send.at[away - 1],
            recv_sem=out_recv.at[away - 1],
            device_id={"seq": peer},
            device_id_type=MESH,
        )

    def forward(load, step):
        arrive(load, step)
        if step < steps - 1:
            send(load, step + 1)

    first = [(load, step) for step in range(steps) for load in (1, 2)]
    moved = 0
    for away in range(1, shards + 1):
        if away < shards:
            outbox[away - 1] = attend(lax.rem(me + away, shards))
            out_copy(away).start()
        else:
            attended_ref[:, my_columns] = attend(me)
        if away * 4 % shards == 0 and away < shards and moved < 3:
            forward(*first[moved])
            moved += 1
    send_last = False
    for load, step in first[moved:-1]:
        if load == 2 and step >= steps - 2:
            continue
        forward(load, step)
        if step >= steps - 2 and not send_last:
            send(3, 0)
            send_last = True
    for away in range(1, shards):
        out_copy(away).wait_recv()
    for copy in kept:
        copy.wait()
    tile = 2 * width

    def joined(full, pair):
        return jnp.concatenate([full[2 * pair], full[2 * pair + 1]], axis=1)

    for at in range(0, depth, tile):
        cols = slice(at, at + tile)
        after[:, cols] = hidden[:, cols].astype(jnp.float32) + jnp.dot(
            attended_ref[...], joined(full_a_ref, at // tile), preferred_element_type=jnp.float32
        )
    conv_normed = layer_norm(after[...]).astype(jnp.bfloat16)
    part = w_b_ref.shape[1]

    def gate(owner):
        at = pl.ds(pl.multiple_of(owner * part, 128), part)
        gates[:, at] = jnp.dot(
            conv_normed, full_b_ref[owner], preferred_element_type=jnp.float32
        )

    def gate_step(step):
        gate(ring_index(place - 1 - step, shards))
        if step < steps - 1:
            gate(ring_index(place + 1 + step, shards))

    gate(me)
    for step in range(steps - 2):
        gate_step(step)
    forward(2, steps - 2)
    gate_step(steps - 2)
    forward(3, 0)
    forward(2, steps - 1)
    gate_step(steps - 1)
    glu = (gates[:, :depth] * jax.nn.sigmoid(gates[:, depth:])).astype(jnp.bfloat16)
    margin = edge.shape[1]
    edge[0] = glu[:margin]
    edge[1] = glu[rows - margin :]

    def edge_copy(side):
        peer = lax.rem(me + (shards - 1 if side == 0 else 1), shards)
        return pltpu.make_async_remote_copy(
            src_ref=edge.at[side],
            dst_ref=edge.at[2 + side],
            send_sem=edge_send.at[side],
            recv_sem=edge_recv.at[side],
            device_id={"seq": peer},
            device_id_type=MESH,
        )

    edge_copy(0).start()
    edge_copy(1).start()
    padded[margin : margin + rows, :] = glu.astype(jnp.float32)
    edge_copy(0).wait_recv()
    edge_copy(1).wait_recv()
    padded[:margin, :] = edge[3].astype(jnp.float32)
    padded[margin + rows :, :] = edge[2].astype(jnp.float32)
    moved_last = 1
    reach = KERNEL // 2

    def taps_of(at):
        own = near_ref[margin : margin + rows, :]
        summed = jnp.zeros((rows, 128), jnp.float32)
        for offset in range(KERNEL):
            start = margin - reach + offset
            term = padded[start : start + rows, at : at + 128] * taps_ref[offset : offset + 1, at : at + 128]
            keep = near_ref[start : start + rows, :] == own
            summed = summed + jnp.where(keep, term, 0.0)
        depthwise[:, at : at + 128] = summed

    for at in range(0, depth, 128):
        taps_of(at)
        if at + 128 == depth // 2 and moved_last < steps - 1:
            forward(3, moved_last)
            moved_last += 1
    conv_act = layer_norm(depthwise[...])
    conv_act = (conv_act * jax.nn.sigmoid(conv_act)).astype(jnp.bfloat16)

    def leave(piece, owner):
        cols = pl.ds(pl.multiple_of(owner * width, 128), width)
        return pltpu.make_async_remote_copy(
            src_ref=leaving.at[:, cols],
            dst_ref=handed_ref.at[:, cols],
            send_sem=leave_send.at[piece],
            recv_sem=leave_recv.at[piece],
            device_id={"phase": phase_next},
            device_id_type=MESH,
        )

    sent = []

    def finish(owner):
        cols = pl.ds(pl.multiple_of(owner * width, 128), width)
        leaving[:, cols] = (
            after[:, cols]
            + jnp.dot(conv_act, full_c_ref[owner], preferred_element_type=jnp.float32)
        ).astype(jnp.bfloat16)
        copy = leave(len(sent), owner)
        copy.start()
        sent.append(copy)

    finish(me)
    for step in range(steps):
        if step >= moved_last:
            forward(3, step)
        finish(ring_index(place - 1 - step, shards))
        if step < steps - 1:
            finish(ring_index(place + 1 + step, shards))
    for away in range(1, shards):
        out_copy(away).wait_send()
    edge_copy(0).wait_send()
    edge_copy(1).wait_send()
    for load in range(4):
        for step in range(steps):
            for way in range(2):
                hop(load, step, way).wait_send()
    for copy in sent:
        copy.wait()


def block_call(shards, hidden, segments, near, taps, weights):
    rows, depth = hidden.shape
    width = weights[0].shape[1]
    total = rows * shards
    steps = shards // 2
    margin = (near.shape[0] - rows) // 2
    vmem = pl.BlockSpec(memory_space=pltpu.VMEM)
    anywhere = pl.BlockSpec(memory_space=pl.ANY)
    dma = pltpu.SemaphoreType.DMA
    bf16, f32 = jnp.bfloat16, jnp.float32
    return pl.pallas_call(
        functools.partial(block_kernel, shards, depth // HEADS),
        out_shape=jax.ShapeDtypeStruct((rows, depth), bf16),
        in_specs=[anywhere] + [vmem] * 4 + [anywhere] * 6,
        out_specs=vmem,
        scratch_shapes=[
            pltpu.VMEM((rows, depth), bf16),
            pltpu.VMEM((depth, 3 * width), bf16),
        ]
        + [pltpu.VMEM((shards, *w.shape), bf16) for w in weights[3:]]
        + [
            pltpu.VMEM((rows, depth), bf16),
            pltpu.VMEM((rows, depth), f32),
            pltpu.VMEM((rows, 2 * depth), f32),
            pltpu.VMEM((4, margin, depth), bf16),
            pltpu.VMEM((rows + 2 * margin, depth), f32),
            pltpu.VMEM((rows, depth), f32),
            pltpu.VMEM((rows, depth), bf16),
            pltpu.VMEM((total, depth), bf16),
            pltpu.VMEM((total, width), bf16),
            pltpu.VMEM((total, width), bf16),
            pltpu.VMEM((total, width), bf16),
            pltpu.VMEM((shards - 1, rows, width), bf16),
            dma((4, steps, 2)),
            dma((4, steps, 2)),
            dma((3,)),
            dma((shards - 1,)),
            dma((shards - 1,)),
            dma((4,)),
            dma((2,)),
            dma((2,)),
            dma((shards,)),
            dma((shards,)),
        ],
        compiler_params=pltpu.CompilerParams(
            collective_id=0, has_side_effects=True, vmem_limit_bytes=56 * 1024 * 1024
        ),
    )(hidden, segments[:, None], segments[None, :], near, taps, *weights)


def attention_general(hidden, utt_lengths, w_query, w_key, w_value, w_output, conv_in, conv_out):
    shards = lax.axis_size("seq")
    my_index = lax.axis_index("seq")
    local_rows = hidden.shape[0]
    width = hidden.shape[1]
    total_rows = local_rows * shards
    head_size = width // HEADS
    scale = 1.0 / math.sqrt(head_size)
    groups = min(HEADS, shards)
    group_heads = HEADS // groups
    parts = shards // groups
    part_rows = local_rows // parts
    group_width = group_heads * head_size
    full_query, full_key, full_value, full_output, full_conv_in, full_conv_out = (
        lax.all_gather(w_query, "seq", axis=1, tiled=True),
        lax.all_gather(w_key, "seq", axis=1, tiled=True),
        lax.all_gather(w_value, "seq", axis=1, tiled=True),
        lax.all_gather(w_output, "seq", axis=1, tiled=True),
        lax.all_gather(conv_in, "seq", axis=1, tiled=True),
        lax.all_gather(conv_out, "seq", axis=1, tiled=True),
    )
    normed = layer_norm(hidden.astype(jnp.float32)).astype(jnp.bfloat16)
    query = jnp.dot(normed, full_query, preferred_element_type=jnp.float32).astype(jnp.bfloat16)
    key_proj = jnp.dot(normed, full_key, preferred_element_type=jnp.float32).astype(jnp.bfloat16)
    value_proj = jnp.dot(normed, full_value, preferred_element_type=jnp.float32).astype(
        jnp.bfloat16
    )
    shaped = query.reshape(parts, part_rows, groups, group_width).transpose(2, 0, 1, 3)
    query_pieces = shaped.reshape(shards, part_rows, group_width)
    kv_local = jnp.concatenate(
        [
            key_proj.reshape(local_rows, groups, group_width),
            value_proj.reshape(local_rows, groups, group_width),
        ],
        axis=2,
    )
    copies = jnp.broadcast_to(
        kv_local.transpose(1, 0, 2)[:, None], (groups, parts, local_rows, 2 * group_width)
    )
    copies = copies.reshape(shards, local_rows, 2 * group_width)
    query_got, kv_got = (
        lax.all_to_all(query_pieces, "seq", split_axis=0, concat_axis=0, tiled=True),
        lax.all_to_all(copies, "seq", split_axis=0, concat_axis=0, tiled=True),
    )
    key_value = kv_got.reshape(total_rows, 2 * group_width)
    count = shards * part_rows
    my_part = my_index % parts
    row_ids = jnp.arange(count, dtype=jnp.int32)
    query_pos = row_ids // part_rows * local_rows + my_part * part_rows + row_ids % part_rows
    queries = query_got.reshape(count, group_heads, head_size)
    key_rows = key_value[:, :group_width].reshape(total_rows, group_heads, head_size)
    value_rows = key_value[:, group_width:].reshape(total_rows, group_heads, head_size)
    seg_all = segment_ids(jnp.arange(total_rows, dtype=jnp.int32), utt_lengths)
    seg_query = segment_ids(query_pos, utt_lengths)
    query_block = math.gcd(512, count)
    blocks = count // query_block

    def attend_block(operands):
        block_query, block_seg = operands
        scores = (
            jnp.einsum("qhd,khd->hqk", block_query, key_rows, preferred_element_type=jnp.float32)
            * scale
        )
        allowed = (block_seg[:, None] == seg_all[None, :])[None]
        scores = jnp.where(allowed, scores, -1e30)
        peak = jnp.max(scores, axis=2, keepdims=True)
        expw = jnp.where(allowed, jnp.exp(scores - peak), 0.0)
        total_weight = jnp.sum(expw, axis=2)
        mixed = jnp.einsum(
            "hqk,khd->hqd",
            expw.astype(jnp.bfloat16),
            value_rows,
            preferred_element_type=jnp.float32,
        )
        mixed = mixed / total_weight[:, :, None]
        return mixed.transpose(1, 0, 2).astype(jnp.bfloat16)

    attended = lax.map(
        attend_block,
        (
            queries.reshape(blocks, query_block, group_heads, head_size),
            seg_query.reshape(blocks, query_block),
        ),
    )
    outgoing = attended.reshape(shards, part_rows, group_width)
    returned = lax.all_to_all(outgoing, "seq", split_axis=0, concat_axis=0, tiled=True)
    attended_local = (
        returned.reshape(groups, parts, part_rows, group_width)
        .transpose(1, 2, 0, 3)
        .reshape(local_rows, width)
    )
    return attended_local, full_output, full_conv_in, full_conv_out


def body(frames, lengths, w_query, w_key, w_value, w_output, conv_in, conv_taps, conv_out):
    hidden = frames[0]
    utt_lengths = lengths[0]
    shards = lax.axis_size("seq")
    my_index = lax.axis_index("seq")
    local_rows = hidden.shape[0]
    width = hidden.shape[1]
    total_rows = local_rows * shards
    phases = lax.axis_size("phase")
    if phases > 2 and shards % 8 == 0 and width // shards == 128 and local_rows % 32 == 0:
        segments = segment_ids(jnp.arange(total_rows, dtype=jnp.int32), utt_lengths)
        margin = 16
        near_pos = my_index * local_rows - margin
        near_pos = near_pos + jnp.arange(local_rows + 2 * margin, dtype=jnp.int32)
        inside = (near_pos >= 0) & (near_pos < total_rows)
        near = jnp.where(inside, segment_ids(near_pos, utt_lengths), -1)
        handed = block_call(
            shards,
            hidden,
            segments,
            jnp.broadcast_to(near[:, None], (near.shape[0], 128)),
            conv_taps[0].astype(jnp.float32),
            (w_query[0], w_key[0], w_value[0], w_output[0], conv_in[0], conv_out[0]),
        )
        return handed[None]
    attended_local, full_output, full_conv_in, full_conv_out = attention_general(
        hidden, utt_lengths, w_query[0], w_key[0], w_value[0], w_output[0], conv_in[0], conv_out[0]
    )
    after_attn = hidden.astype(jnp.float32) + jnp.dot(
        attended_local, full_output, preferred_element_type=jnp.float32
    )
    conv_normed = layer_norm(after_attn).astype(jnp.bfloat16)
    gates = jnp.dot(conv_normed, full_conv_in, preferred_element_type=jnp.float32)
    glu = (gates[:, :width] * jax.nn.sigmoid(gates[:, width:])).astype(jnp.bfloat16)
    reach = KERNEL // 2
    padded = padded_2(glu, (("seq", 0),), KERNEL // 2)
    padded_pos = my_index * local_rows - reach + jnp.arange(local_rows + 2 * reach, dtype=jnp.int32)
    inside = (padded_pos >= 0) & (padded_pos < total_rows)
    padded_seg = jnp.where(inside, segment_ids(padded_pos, utt_lengths), -1)
    own_seg = padded_seg[reach : reach + local_rows]
    taps = conv_taps[0]
    depthwise = jnp.zeros((local_rows, width), jnp.float32)
    for offset in range(KERNEL):
        keep = padded_seg[offset : offset + local_rows] == own_seg
        term = padded[offset : offset + local_rows].astype(jnp.float32) * taps[offset].astype(
            jnp.float32
        )
        depthwise = depthwise + jnp.where(keep[:, None], term, 0.0)
    conv_act = layer_norm(depthwise)
    conv_act = (conv_act * jax.nn.sigmoid(conv_act)).astype(jnp.bfloat16)
    block_out = (
        after_attn + jnp.dot(conv_act, full_conv_out, preferred_element_type=jnp.float32)
    ).astype(jnp.bfloat16)
    passed = passed_along(block_out, "phase", 1)
    return passed[None]


def solution(mesh):
    in_specs = (
        P("phase", "seq", None),
        P("phase", None),
        P("phase", None, "seq"),
        P("phase", None, "seq"),
        P("phase", None, "seq"),
        P("phase", None, "seq"),
        P("phase", None, "seq"),
        P("phase", None, None),
        P("phase", None, "seq"),
    )
    out_specs = P("phase", "seq", None)
    return jax.shard_map(body, mesh=mesh, in_specs=in_specs, out_specs=out_specs, check_vma=False)
```

profile of v0, /device:TPU:1, one launch (start us, length us, event | category | flops | bytes accessed | tf_op | source)
XLA Modules:
  0.0 136.6 jit_solution(745308908185984217)
XLA Ops:
  0.0 0.0 copy-start.1
  0.0 0.7 copy-done.1
  0.7 0.0 copy-start
  0.7 0.1 select_reduce_fusion
  0.8 0.1 convert_reduce_fusion.1
  0.9 0.1 convert_reduce_fusion
  1.0 0.6 broadcast_in_dim.49.seg_col_ref
  1.6 0.7 broadcast_in_dim.51.near_ref
  2.3 0.0 copy-done
  2.3 0.7 bitcast_convert_fusion.taps_ref
  3.0 1.1 broadcast_in_dim.53.seg_row_ref
  4.0 130.8 %shard_map.91 = bf16[160,1024]{1,0:T(8,128)(2,1)} custom-call(bf16[160,1024]{1,0:T(8,128)(2,1)} %bitcast.14, s32[1280,1]{1,0:T(8,128)} %broadcast_in_dim.53.seg_row_ref, s32[1,1280]{1,0:T(1,128)} %broadcast_in_dim.49.seg_col_ref, s32[192,128]{1,0:T(8,128)} %broadcast_in_dim.51.near_ref, f32[31,1024]{1,0:T(8,128)} %bitcast_convert_fusion.taps_ref, ...), custom_call_target="tpu_custom_call" | custom-call | tf_op jit(solution)/shard_map/pallas_call | solution.py:388
  134.8 1.7 %copy.13 = bf16[1,160,1024]{2,1,0:T(8,128)(2,1)} copy(bf16[1,160,1024]{2,1,0:T(8,128)(2,1)} %bitcast.12) | data formatting | bytes 655360
  (2 shorter events, 0.0 us)
Async XLA Ops:
  0.0 0.7 copy-start.1
  0.7 1.6 %copy-start = (bf16[1,31,1024]{2,1,0:T(8,128)(2,1)S(1)}, bf16[1,31,1024]{2,1,0:T(8,128)(2,1)}, u32[]{:S(2)}) copy-start(bf16[1,31,1024]{2,1,0:T(8,128)(2,1)} %param.16) | copy-start | bytes 190468
where the time goes:
time: 137 us
  Pallas kernels  131 us (96%)
  local copies, waits for them, and re-layouts  4.76 us (3%)
    pallas_call x1, Pallas kernels, block_call(): pl.pallas_call(functools.partial(block_kernel, shards, depth // HEADS), o...  131 us

commit v1 on v0

--- a/solution.py
+++ b/solution.py
@@ -50,13 +50,18 @@
     return (1 - late) * (2 * place) + late * (2 * (shards - 1 - place) + 1)
 
 
+def segment_of(positions, bounds):
+    segment = jnp.zeros(positions.shape, jnp.int32)
+    for bound in bounds:
+        segment = segment + (positions >= bound).astype(jnp.int32)
+    return segment
+
+
 def block_kernel(
     shards,
     head_size,
+    lengths_ref,
     frames_ref,
-    seg_row_ref,
-    seg_col_ref,
-    near_ref,
     taps_ref,
     query_ref,
     key_ref,
@@ -68,14 +73,17 @@
     hidden,
     qkv,
     full_a_ref,
-    full_b_ref,
+    half_b_ref,
     full_c_ref,
     attended_ref,
     after,
-    gates,
-    edge,
+    conv_rows,
+    near,
+    taps,
     padded,
     depthwise,
+    deep_out,
+    deep_in,
     leaving,
     normed,
     query,
@@ -88,8 +96,14 @@
     out_send,
     out_recv,
     in_sem,
+    b_send,
+    b_recv,
+    rows_send,
+    rows_recv,
     edge_send,
     edge_recv,
+    deep_send,
+    deep_recv,
     leave_send,
     leave_recv,
 ):
@@ -108,6 +122,15 @@
     odd = lax.rem(me, 2)
     place = (1 - odd) * lax.div(me, 2) + odd * (shards - 1 - lax.div(me, 2))
     right, left = ring_index(place + 1, shards), ring_index(place - 1, shards)
+    half = lax.rem(lax.div(me, 2), 2)
+    upper = lax.div(me, 4)
+
+    def partner_of(owner):
+        return owner + 2 - 4 * lax.rem(lax.div(owner, 2), 2)
+
+    beside = me + 1 - 2 * odd
+    across = me + 4 - 8 * upper
+    partner = partner_of(me)
 
     barrier = pltpu.get_barrier_semaphore()
     for away in range(1, shards):
@@ -125,43 +148,43 @@
     normed[own_rows, :] = layer_norm(hidden[...].astype(jnp.float32)).astype(jnp.bfloat16)
     pl.semaphore_wait(barrier, shards + 1)
 
-    pairs = ((w_a_ref, full_a_ref), (w_b_ref, full_b_ref), (w_c_ref, full_c_ref))
-
-    def view(load, owner, half):
+    rings = {1: (w_a_ref, full_a_ref), 2: (w_c_ref, full_c_ref)}
+
+    def hop(load, step, way, piece):
+        owner = ring_index(place - step if way == 0 else place + step, shards)
         if load == 0:
-            first, size = (0, rows) if half is None else (half * (rows // 2), rows // 2)
-            return normed.at[pl.ds(pl.multiple_of(owner * rows + first, 16), size), :]
-        own, full = pairs[load - 1]
-        depth = own.shape[0]
-        first, size = (0, depth) if half is None else (half * (depth // 2), depth // 2)
-        return full.at[owner, pl.ds(first, size), :]
-
-    def hop(load, step, way):
-        half = way if step == steps - 1 else None
-        owner = ring_index(place - step if way == 0 else place + step, shards)
-        target = view(load, owner, half)
-        source = target
-        if load > 0 and step == 0:
-            source = pairs[load - 1][0]
-            if half is not None:
-                depth = source.shape[0] // 2
-                source = source.at[pl.ds(half * depth, depth), :]
+            size = rows // 2
+            first = pl.multiple_of(owner * rows + piece * size, 16)
+            source = target = normed.at[pl.ds(first, size), :]
+        else:
+            own, full = rings[load]
+            size = own.shape[0] // 2
+            target = full.at[owner, pl.ds(piece * size, size), :]
+            source = own.at[pl.ds(piece * size, size), :] if step == 0 else target
+        at = (load * steps + step) * 2 + way
         return pltpu.make_async_remote_copy(
             src_ref=source,
             dst_ref=target,
-            send_sem=send_sem.at[load, step, way],
-            recv_sem=recv_sem.at[load, step, way],
+            send_sem=send_sem.at[at, piece],
+            recv_sem=recv_sem.at[at, piece],
             device_id={"seq": right if way == 0 else left},
             device_id_type=MESH,
         )
 
-    def arrive(load, step):
-        for way in range(2):
-            hop(load, step, way).wait_recv()
-
-    def send(load, step):
-        for way in range(2):
-            hop(load, step, way).start()
+    def hops(step):
+        pairs = [(way, piece) for piece in range(2) for way in range(2)]
+        return [(way, piece) for way, piece in pairs if step < steps - 1 or way == piece]
+
+    def send(load):
+        for way, piece in hops(0):
+            hop(load, 0, way, piece).start()
+
+    def forward(load, step):
+        onward = hops(step + 1) if step < steps - 1 else ()
+        for way, piece in hops(step):
+            hop(load, step, way, piece).wait_recv()
+            if (way, piece) in onward:
+                hop(load, step + 1, way, piece).start()
 
     def project(owner):
         at = pl.ds(pl.multiple_of(owner * rows, rows), rows)
@@ -171,23 +194,49 @@
         keys[at, :] = both[:, width : 2 * width]
         values[at, :] = both[:, 2 * width :]
 
-    kept = []
-    send(0, 0)
-    for load in (1, 2, 3):
-        own, full = pairs[load - 1]
-        copy = pltpu.make_async_copy(own, full.at[me], own_sem.at[load - 1])
+    def b_slot(owner):
+        return lax.div(owner, 4) * 2 + lax.rem(owner, 2)
+
+    def b_copy(kind, piece):
+        size = w_b_ref.shape[0] // 2
+        at = pl.ds(piece * size, size)
+        slot = b_slot(across if kind == 2 else me)
+        target = half_b_ref.at[slot, at, :]
+        return pltpu.make_async_remote_copy(
+            src_ref=target if kind == 2 else w_b_ref.at[at, :],
+            dst_ref=target,
+            send_sem=b_send.at[kind, piece],
+            recv_sem=b_recv.at[kind, piece],
+            device_id={"seq": across if kind == 0 else beside},
+            device_id_type=MESH,
+        )
+
+    send(0)
+    kept = [
+        pltpu.make_async_copy(w_a_ref, full_a_ref.at[me], own_sem.at[0]),
+        pltpu.make_async_copy(w_b_ref, half_b_ref.at[b_slot(me)], own_sem.at[1]),
+        pltpu.make_async_copy(w_c_ref, full_c_ref.at[me], own_sem.at[2]),
+    ]
+    for copy in kept:
         copy.start()
-        kept.append(copy)
+
+    bounds = [lengths_ref[0]]
+    for utt in range(1, lengths_ref.shape[0]):
+        bounds.append(bounds[-1] + lengths_ref[utt])
+    seg_col = segment_of(lax.broadcasted_iota(jnp.int32, (1, rows * shards), 1), bounds)
+    margin = (near.shape[1] - rows) // 2
+    for slot, owner in enumerate((me, partner)):
+        positions = lax.broadcasted_iota(jnp.int32, near.shape[1:], 0) + (owner * rows - margin)
+        near[slot] = jnp.where(positions >= 0, segment_of(positions, bounds), -1)
+    taps[...] = taps_ref[...].astype(jnp.float32)
+
     for copy in loads_in[1:]:
         copy.wait()
     project(me)
     for step in range(steps):
-        arrive(0, step)
-        if step < steps - 1:
-            send(0, step + 1)
+        forward(0, step)
         if step == steps - 2:
-            send(1, 0)
-            send(2, 0)
+            send(1)
         project(ring_index(place - 1 - step, shards))
         if step < steps - 1:
             project(ring_index(place + 1 + step, shards))
@@ -198,7 +247,8 @@
     def attend(owner):
         at = pl.ds(pl.multiple_of(owner * rows, rows), rows)
         block = query[at, :]
-        allowed = seg_row_ref[at, :] == seg_col_ref[...]
+        positions = lax.broadcasted_iota(jnp.int32, (rows, 1), 0) + owner * rows
+        allowed = segment_of(positions, bounds) == seg_col
         result = jnp.zeros((rows, width), jnp.float32)
         for head in range(width // head_size):
             mine = (lane >= head * head_size) & (lane < (head + 1) * head_size)
@@ -229,34 +279,24 @@
             device_id_type=MESH,
         )
 
-    def forward(load, step):
-        arrive(load, step)
-        if step < steps - 1:
-            send(load, step + 1)
-
-    first = [(load, step) for step in range(steps) for load in (1, 2)]
-    moved = 0
     for away in range(1, shards + 1):
         if away < shards:
             outbox[away - 1] = attend(lax.rem(me + away, shards))
             out_copy(away).start()
         else:
             attended_ref[:, my_columns] = attend(me)
-        if away * 4 % shards == 0 and away < shards and moved < 3:
-            forward(*first[moved])
-            moved += 1
-    send_last = False
-    for load, step in first[moved:-1]:
-        if load == 2 and step >= steps - 2:
-            continue
-        forward(load, step)
-        if step >= steps - 2 and not send_last:
-            send(3, 0)
-            send_last = True
+        if away == 4:
+            forward(1, 0)
+    forward(1, 1)
+    for piece in range(2):
+        b_copy(0, piece).start()
+    for piece in range(2):
+        b_copy(1, piece).start()
+    forward(1, 2)
     for away in range(1, shards):
         out_copy(away).wait_recv()
-    for copy in kept:
-        copy.wait()
+    kept[0].wait()
+    forward(1, 3)
     tile = 2 * width
 
     def joined(full, pair):
@@ -267,69 +307,102 @@
         after[:, cols] = hidden[:, cols].astype(jnp.float32) + jnp.dot(
             attended_ref[...], joined(full_a_ref, at // tile), preferred_element_type=jnp.float32
         )
-    conv_normed = layer_norm(after[...]).astype(jnp.bfloat16)
+    conv_rows[0, margin : margin + rows, :] = layer_norm(after[...]).astype(jnp.bfloat16)
+
+    rows_copy = pltpu.make_async_remote_copy(
+        src_ref=conv_rows.at[0, pl.ds(margin, rows), :],
+        dst_ref=conv_rows.at[1, pl.ds(margin, rows), :],
+        send_sem=rows_send,
+        recv_sem=rows_recv,
+        device_id={"seq": partner},
+        device_id_type=MESH,
+    )
+    rows_copy.start()
+
+    def edge_copy(side, slot):
+        owner = lax.rem(me + (1 if side == 0 else shards - 1), shards)
+        first, at = (rows, 0) if side == 0 else (margin, margin + rows)
+        return pltpu.make_async_remote_copy(
+            src_ref=conv_rows.at[0, pl.ds(first, margin), :],
+            dst_ref=conv_rows.at[slot, pl.ds(at, margin), :],
+            send_sem=edge_send.at[side, slot],
+            recv_sem=edge_recv.at[side, slot],
+            device_id={"seq": owner if slot == 0 else partner_of(owner)},
+            device_id_type=MESH,
+        )
+
+    edges = [edge_copy(side, slot) for slot in range(2) for side in range(2)]
+    for copy in edges:
+        copy.start()
+    for piece in range(2):
+        b_copy(0, piece).wait_recv()
+        b_copy(2, piece).start()
+    send(2)
+    kept[1].wait()
+    rows_copy.wait_recv()
+    for copy in edges:
+        copy.wait_recv()
+
     part = w_b_ref.shape[1]
-
-    def gate(owner):
-        at = pl.ds(pl.multiple_of(owner * part, 128), part)
-        gates[:, at] = jnp.dot(
-            conv_normed, full_b_ref[owner], preferred_element_type=jnp.float32
-        )
-
-    def gate_step(step):
-        gate(ring_index(place - 1 - step, shards))
-        if step < steps - 1:
-            gate(ring_index(place + 1 + step, shards))
-
-    gate(me)
-    for step in range(steps - 2):
-        gate_step(step)
-    forward(2, steps - 2)
-    gate_step(steps - 2)
-    forward(3, 0)
-    forward(2, steps - 1)
-    gate_step(steps - 1)
-    glu = (gates[:, :depth] * jax.nn.sigmoid(gates[:, depth:])).astype(jnp.bfloat16)
-    margin = edge.shape[1]
-    edge[0] = glu[:margin]
-    edge[1] = glu[rows - margin :]
-
-    def edge_copy(side):
-        peer = lax.rem(me + (shards - 1 if side == 0 else 1), shards)
-        return pltpu.make_async_remote_copy(
-            src_ref=edge.at[side],
-            dst_ref=edge.at[2 + side],
-            send_sem=edge_send.at[side],
-            recv_sem=edge_recv.at[side],
-            device_id={"seq": peer},
-            device_id_type=MESH,
-        )
-
-    edge_copy(0).start()
-    edge_copy(1).start()
-    padded[margin : margin + rows, :] = glu.astype(jnp.float32)
-    edge_copy(0).wait_recv()
-    edge_copy(1).wait_recv()
-    padded[:margin, :] = edge[3].astype(jnp.float32)
-    padded[margin + rows :, :] = edge[2].astype(jnp.float32)
-    moved_last = 1
     reach = KERNEL // 2
 
-    def taps_of(at):
-        own = near_ref[margin : margin + rows, :]
+    def gate(piece):
+        for slot in range(2):
+            block = conv_rows[slot]
+            value = jnp.dot(block, half_b_ref[piece], preferred_element_type=jnp.float32)
+            gates = jnp.dot(block, half_b_ref[2 + piece], preferred_element_type=jnp.float32)
+            glu = (value * jax.nn.sigmoid(gates)).astype(jnp.bfloat16)
+            padded[slot] = glu.astype(jnp.float32)
+
+    def taps_of(piece, slot, at):
+        cols = pl.ds(pl.multiple_of(half * (2 * part) + piece * part + at, 128), 128)
+        block = taps[:, cols]
+        own = near[slot, margin : margin + rows, :]
         summed = jnp.zeros((rows, 128), jnp.float32)
         for offset in range(KERNEL):
             start = margin - reach + offset
-            term = padded[start : start + rows, at : at + 128] * taps_ref[offset : offset + 1, at : at + 128]
-            keep = near_ref[start : start + rows, :] == own
+            term = padded[slot, start : start + rows, at : at + 128] * block[offset : offset + 1]
+            keep = near[slot, start : start + rows, :] == own
             summed = summed + jnp.where(keep, term, 0.0)
-        depthwise[:, at : at + 128] = summed
-
-    for at in range(0, depth, 128):
-        taps_of(at)
-        if at + 128 == depth // 2 and moved_last < steps - 1:
-            forward(3, moved_last)
-            moved_last += 1
+        if slot == 0:
+            depthwise[:, cols] = summed
+        else:
+            deep_out[:, pl.ds(pl.multiple_of(piece * part + at, 128), 128)] = summed.astype(
+                jnp.bfloat16
+            )
+
+    def deep_copy(order):
+        piece = odd if order == 0 else 1 - odd
+        cols = pl.ds(pl.multiple_of(piece * part, 128), part)
+        return pltpu.make_async_remote_copy(
+            src_ref=deep_out.at[:, cols],
+            dst_ref=deep_in.at[:, cols],
+            send_sem=deep_send.at[order],
+            recv_sem=deep_recv.at[order],
+            device_id={"seq": partner},
+            device_id_type=MESH,
+        )
+
+    def convolve(order):
+        piece = odd if order == 0 else 1 - odd
+        gate(piece)
+        for at in range(0, part, 128):
+            taps_of(piece, 1, at)
+        deep_copy(order).start()
+        for at in range(0, part, 128):
+            taps_of(piece, 0, at)
+
+    convolve(0)
+    forward(2, 0)
+    for kind in (1, 2):
+        for piece in range(2):
+            b_copy(kind, piece).wait_recv()
+    convolve(1)
+    forward(2, 1)
+    for order in range(2):
+        deep_copy(order).wait_recv()
+    other = pl.ds(pl.multiple_of((1 - half) * (2 * part), 128), 2 * part)
+    depthwise[:, other] = deep_in[...].astype(jnp.float32)
     conv_act = layer_norm(depthwise[...])
     conv_act = (conv_act * jax.nn.sigmoid(conv_act)).astype(jnp.bfloat16)
 
@@ -356,64 +429,82 @@
         copy.start()
         sent.append(copy)
 
+    kept[2].wait()
     finish(me)
     for step in range(steps):
-        if step >= moved_last:
-            forward(3, step)
+        if step >= 2:
+            forward(2, step)
         finish(ring_index(place - 1 - step, shards))
         if step < steps - 1:
             finish(ring_index(place + 1 + step, shards))
     for away in range(1, shards):
         out_copy(away).wait_send()
-    edge_copy(0).wait_send()
-    edge_copy(1).wait_send()
-    for load in range(4):
+    rows_copy.wait_send()
+    for copy in edges:
+        copy.wait_send()
+    for order in range(2):
+        deep_copy(order).wait_send()
+    for kind in range(3):
+        for piece in range(2):
+            b_copy(kind, piece).wait_send()
+    for load in range(3):
         for step in range(steps):
-            for way in range(2):
-                hop(load, step, way).wait_send()
+            for way, piece in hops(step):
+                hop(load, step, way, piece).wait_send()
     for copy in sent:
         copy.wait()
 
 
-def block_call(shards, hidden, segments, near, taps, weights):
+def block_call(shards, hidden, lengths, taps, weights):
     rows, depth = hidden.shape
     width = weights[0].shape[1]
+    part = weights[4].shape[1]
     total = rows * shards
     steps = shards // 2
-    margin = (near.shape[0] - rows) // 2
+    margin = 16
     vmem = pl.BlockSpec(memory_space=pltpu.VMEM)
+    smem = pl.BlockSpec(memory_space=pltpu.SMEM)
     anywhere = pl.BlockSpec(memory_space=pl.ANY)
     dma = pltpu.SemaphoreType.DMA
     bf16, f32 = jnp.bfloat16, jnp.float32
     return pl.pallas_call(
         functools.partial(block_kernel, shards, depth // HEADS),
         out_shape=jax.ShapeDtypeStruct((rows, depth), bf16),
-        in_specs=[anywhere] + [vmem] * 4 + [anywhere] * 6,
+        in_specs=[smem, anywhere, vmem] + [anywhere] * 6,
         out_specs=vmem,
         scratch_shapes=[
             pltpu.VMEM((rows, depth), bf16),
             pltpu.VMEM((depth, 3 * width), bf16),
-        ]
-        + [pltpu.VMEM((shards, *w.shape), bf16) for w in weights[3:]]
-        + [
+            pltpu.VMEM((shards, depth, width), bf16),
+            pltpu.VMEM((shards // 2, depth, part), bf16),
+            pltpu.VMEM((shards, depth, width), bf16),
             pltpu.VMEM((rows, depth), bf16),
             pltpu.VMEM((rows, depth), f32),
-            pltpu.VMEM((rows, 2 * depth), f32),
-            pltpu.VMEM((4, margin, depth), bf16),
-            pltpu.VMEM((rows + 2 * margin, depth), f32),
+            pltpu.VMEM((2, rows + 2 * margin, depth), bf16),
+            pltpu.VMEM((2, rows + 2 * margin, 128), jnp.int32),
+            pltpu.VMEM(taps.shape, f32),
+            pltpu.VMEM((2, rows + 2 * margin, part), f32),
             pltpu.VMEM((rows, depth), f32),
+            pltpu.VMEM((rows, depth // 2), bf16),
+            pltpu.VMEM((rows, depth // 2), bf16),
             pltpu.VMEM((rows, depth), bf16),
             pltpu.VMEM((total, depth), bf16),
             pltpu.VMEM((total, width), bf16),
             pltpu.VMEM((total, width), bf16),
             pltpu.VMEM((total, width), bf16),
             pltpu.VMEM((shards - 1, rows, width), bf16),
-            dma((4, steps, 2)),
-            dma((4, steps, 2)),
+            dma((3 * steps * 2, 2)),
+            dma((3 * steps * 2, 2)),
             dma((3,)),
             dma((shards - 1,)),
             dma((shards - 1,)),
             dma((4,)),
+            dma((3, 2)),
+            dma((3, 2)),
+            dma,
+            dma,
+            dma((2, 2)),
+            dma((2, 2)),
             dma((2,)),
             dma((2,)),
             dma((shards,)),
@@ -422,7 +513,7 @@
         compiler_params=pltpu.CompilerParams(
             collective_id=0, has_side_effects=True, vmem_limit_bytes=56 * 1024 * 1024
         ),
-    )(hidden, segments[:, None], segments[None, :], near, taps, *weights)
+    )(lengths, hidden, taps, *weights)
 
 
 def attention_general(hidden, utt_lengths, w_query, w_key, w_value, w_output, conv_in, conv_out):
@@ -528,22 +619,9 @@
     width = hidden.shape[1]
     total_rows = local_rows * shards
     phases = lax.axis_size("phase")
-    if phases > 2 and shards % 8 == 0 and width // shards == 128 and local_rows % 32 == 0:
-        segments = segment_ids(jnp.arange(total_rows, dtype=jnp.int32), utt_lengths)
-        margin = 16
-        near_pos = my_index * local_rows - margin
-        near_pos = near_pos + jnp.arange(local_rows + 2 * margin, dtype=jnp.int32)
-        inside = (near_pos >= 0) & (near_pos < total_rows)
-        near = jnp.where(inside, segment_ids(near_pos, utt_lengths), -1)
-        handed = block_call(
-            shards,
-            hidden,
-            segments,
-            jnp.broadcast_to(near[:, None], (near.shape[0], 128)),
-            conv_taps[0].astype(jnp.float32),
-            (w_query[0], w_key[0], w_value[0], w_output[0], conv_in[0], conv_out[0]),
-        )
-        return handed[None]
+    if phases > 2 and shards == 8 and width // shards == 128 and local_rows % 32 == 0:
+        weights = (w_query[0], w_key[0], w_value[0], w_output[0], conv_in[0], conv_out[0])
+        return block_call(shards, hidden, utt_lengths, conv_taps[0], weights)[None]
     attended_local, full_output, full_conv_in, full_conv_out = attention_general(
         hidden, utt_lengths, w_query[0], w_key[0], w_value[0], w_output[0], conv_in[0], conv_out[0]
     )

time: 137 us -> 122 us (0.89)
  Pallas kernels: 131 us -> 120 us
  local copies, waits for them, and re-layouts: 4.76 us -> 1.72 us
    pallas_call x1, Pallas kernels: 131 us -> 120 us  [block_call(): pl.pallas_call(functools.partial(block_kernel, shards, depth // HEADS), o...]
    broadcast_in_dim x3 -> x0, local copies, waits for them, and re-layouts: 2.39 us -> none  [the longest x1 1.07 us: block_call(): segments[:, None]]
where the time goes in v1:
time: 122 us; the launch traced here: 121 us
  Pallas kernels  120 us (98%)
  local copies, waits for them, and re-layouts  1.72 us (1%)
    pallas_call x1, Pallas kernels, block_call(): pl.pallas_call(functools.partial(block_kernel, shards, depth // HEADS), o...  120 us

profile of v1, /device:TPU:1, one launch (start us, length us, event | category | flops | bytes accessed | tf_op | source)
XLA Modules:
  0.0 121.2 jit_solution(2648363666754125693)
XLA Ops:
  0.0 119.5 %shard_map.91 = bf16[160,1024]{1,0:T(8,128)(2,1)} custom-call(s32[8]{0:T(128)} %bitcast.19, bf16[160,1024]{1,0:T(8,128)(2,1)} %bitcast.12, bf16[31,1024]{1,0:T(8,128)(2,1)} %bitcast.18, bf16[1024,128]{1,0:T(8,128)(2,1)} %bitcast.13, bf16[1024,128]{1,0:T(8,128)(2,1)} %bitcast.14, bf16[1024,128]{1,0:T(8,128)(2,1)} %bitcast.15, bf16[1024,128]{1,0:T(8,128)(2,1)} %bitcast.16, ...), custom_call_target="tpu_custom_call" | custom-call | tf_op jit(solution)/shard_map/pallas_call | solution.py:470
  119.5 1.7 %copy.11 = bf16[1,160,1024]{2,1,0:T(8,128)(2,1)} copy(bf16[1,160,1024]{2,1,0:T(8,128)(2,1)} %bitcast.10) | data formatting | bytes 655360

commit v2 on v1

--- a/solution.py
+++ b/solution.py
@@ -84,6 +84,7 @@
     depthwise,
     deep_out,
     deep_in,
+    conv_act,
     leaving,
     normed,
     query,
@@ -96,8 +97,12 @@
     out_send,
     out_recv,
     in_sem,
+    w_send,
+    w_recv,
     b_send,
     b_recv,
+    hidden_send,
+    hidden_recv,
     rows_send,
     rows_recv,
     edge_send,
@@ -110,7 +115,8 @@
     rows = frames_ref.shape[0]
     depth = frames_ref.shape[1]
     width = query_ref.shape[1]
-    loads_in = [pltpu.make_async_copy(frames_ref, hidden, in_sem.at[3])]
+    part = w_b_ref.shape[1]
+    loads_in = [pltpu.make_async_copy(frames_ref, hidden.at[pl.ds(0, rows), :], in_sem.at[3])]
     for i, ref in enumerate((query_ref, key_ref, value_ref)):
         loads_in.append(
             pltpu.make_async_copy(ref, qkv.at[:, pl.ds(i * width, width)], in_sem.at[i])
@@ -128,9 +134,16 @@
     def partner_of(owner):
         return owner + 2 - 4 * lax.rem(lax.div(owner, 2), 2)
 
+    def inner_of(owner):
+        return lax.rem(lax.div(lax.div(owner, 2) + 1, 2), 2)
+
     beside = me + 1 - 2 * odd
     across = me + 4 - 8 * upper
+    facing = me + 2 - 4 * upper
     partner = partner_of(me)
+    inner = inner_of(me) == 1
+    outer = inner_of(me) == 0
+    home = inner_of(me) * me + (1 - inner_of(me)) * partner
 
     barrier = pltpu.get_barrier_semaphore()
     for away in range(1, shards):
@@ -140,51 +153,46 @@
     phases = lax.axis_size("phase")
     phase_next = lax.rem(phase + 1, phases)
     phase_back = lax.rem(phase + phases - 1, phases)
-    for peer in (phase_next, phase_back):
-        pl.semaphore_signal(barrier, inc=1, device_id={"phase": peer}, device_id_type=MESH)
+    for other in (phase_next, phase_back):
+        for peer in (me, partner):
+            pl.semaphore_signal(
+                barrier, inc=1, device_id={"phase": other, "seq": peer}, device_id_type=MESH
+            )
 
     loads_in[0].wait()
     own_rows = pl.ds(pl.multiple_of(me * rows, rows), rows)
-    normed[own_rows, :] = layer_norm(hidden[...].astype(jnp.float32)).astype(jnp.bfloat16)
-    pl.semaphore_wait(barrier, shards + 1)
-
-    rings = {1: (w_a_ref, full_a_ref), 2: (w_c_ref, full_c_ref)}
-
-    def hop(load, step, way, piece):
-        owner = ring_index(place - step if way == 0 else place + step, shards)
-        if load == 0:
-            size = rows // 2
-            first = pl.multiple_of(owner * rows + piece * size, 16)
-            source = target = normed.at[pl.ds(first, size), :]
-        else:
-            own, full = rings[load]
-            size = own.shape[0] // 2
-            target = full.at[owner, pl.ds(piece * size, size), :]
-            source = own.at[pl.ds(piece * size, size), :] if step == 0 else target
-        at = (load * steps + step) * 2 + way
+    normed[own_rows, :] = layer_norm(hidden[:rows, :].astype(jnp.float32)).astype(jnp.bfloat16)
+    pl.semaphore_wait(barrier, shards + 3)
+
+    def remote(source, target, sent, got, peer, onward=None):
+        place_of = {"seq": peer} if onward is None else {"phase": onward, "seq": peer}
         return pltpu.make_async_remote_copy(
             src_ref=source,
             dst_ref=target,
-            send_sem=send_sem.at[at, piece],
-            recv_sem=recv_sem.at[at, piece],
-            device_id={"seq": right if way == 0 else left},
+            send_sem=sent,
+            recv_sem=got,
+            device_id=place_of,
             device_id_type=MESH,
         )
+
+    def hop(step, way, piece):
+        owner = ring_index(place - step if way == 0 else place + step, shards)
+        size = rows // 2
+        block = normed.at[pl.ds(pl.multiple_of(owner * rows + piece * size, 16), size), :]
+        at = step * 2 + way
+        peer = right if way == 0 else left
+        return remote(block, block, send_sem.at[at, piece], recv_sem.at[at, piece], peer)
 
     def hops(step):
         pairs = [(way, piece) for piece in range(2) for way in range(2)]
         return [(way, piece) for way, piece in pairs if step < steps - 1 or way == piece]
 
-    def send(load):
-        for way, piece in hops(0):
-            hop(load, 0, way, piece).start()
-
-    def forward(load, step):
+    def forward(step):
         onward = hops(step + 1) if step < steps - 1 else ()
         for way, piece in hops(step):
-            hop(load, step, way, piece).wait_recv()
+            hop(step, way, piece).wait_recv()
             if (way, piece) in onward:
-                hop(load, step + 1, way, piece).start()
+                hop(step + 1, way, piece).start()
 
     def project(owner):
         at = pl.ds(pl.multiple_of(owner * rows, rows), rows)
@@ -194,31 +202,73 @@
         keys[at, :] = both[:, width : 2 * width]
         values[at, :] = both[:, 2 * width :]
 
+    fulls = ((w_a_ref, full_a_ref), (w_c_ref, full_c_ref))
+    wholes = range(2)
+
+    def chunk(full, owner, first, size):
+        cols = pl.ds(pl.multiple_of(lax.rem(owner, 2) * width, 128), width)
+        return full.at[lax.div(owner, 2), pl.ds(first, size), cols]
+
+    def w_copy(load, kind, piece):
+        own, full = fulls[load]
+        size = depth // 2
+        owner = (me, me, me, partner, partner, facing, partner_of(facing))[kind]
+        peer = (partner, beside, facing, facing, beside, beside, beside)[kind]
+        target = chunk(full, owner, piece * size, size)
+        source = own.at[pl.ds(piece * size, size), :] if kind < 3 else target
+        return remote(
+            source, target, w_send.at[load, kind, piece], w_recv.at[load, kind, piece], peer
+        )
+
+    def w_start(load, kind):
+        for piece in wholes:
+            w_copy(load, kind, piece).start()
+
+    def w_wait(load, kind, then=()):
+        for piece in wholes:
+            w_copy(load, kind, piece).wait_recv()
+            for more in then:
+                w_copy(load, more, piece).start()
+
     def b_slot(owner):
         return lax.div(owner, 4) * 2 + lax.rem(owner, 2)
 
+    b_pieces = range(4)
+
     def b_copy(kind, piece):
-        size = w_b_ref.shape[0] // 2
+        size = depth // len(b_pieces)
         at = pl.ds(piece * size, size)
-        slot = b_slot(across if kind == 2 else me)
-        target = half_b_ref.at[slot, at, :]
-        return pltpu.make_async_remote_copy(
-            src_ref=target if kind == 2 else w_b_ref.at[at, :],
-            dst_ref=target,
-            send_sem=b_send.at[kind, piece],
-            recv_sem=b_recv.at[kind, piece],
-            device_id={"seq": across if kind == 0 else beside},
-            device_id_type=MESH,
-        )
-
-    send(0)
+        target = half_b_ref.at[b_slot(across if kind == 2 else me), at, :]
+        source = target if kind == 2 else w_b_ref.at[at, :]
+        peer = across if kind == 0 else beside
+        return remote(source, target, b_send.at[kind, piece], b_recv.at[kind, piece], peer)
+
+    def b_start(kind):
+        for piece in b_pieces:
+            b_copy(kind, piece).start()
+
+    for way, piece in hops(0):
+        hop(0, way, piece).start()
+
+    @pl.when(inner)
+    def _():
+        w_start(0, 1)
+        b_start(1)
+
     kept = [
-        pltpu.make_async_copy(w_a_ref, full_a_ref.at[me], own_sem.at[0]),
+        pltpu.make_async_copy(w_a_ref, chunk(full_a_ref, me, 0, depth), own_sem.at[0]),
         pltpu.make_async_copy(w_b_ref, half_b_ref.at[b_slot(me)], own_sem.at[1]),
-        pltpu.make_async_copy(w_c_ref, full_c_ref.at[me], own_sem.at[2]),
+        pltpu.make_async_copy(w_c_ref, chunk(full_c_ref, me, 0, depth), own_sem.at[2]),
     ]
     for copy in kept:
         copy.start()
+    hidden_copy = remote(
+        hidden.at[pl.ds(0, rows), :],
+        hidden.at[pl.ds(rows, rows), :],
+        hidden_send,
+        hidden_recv,
+        partner,
+    )
 
     bounds = [lengths_ref[0]]
     for utt in range(1, lengths_ref.shape[0]):
@@ -234,9 +284,18 @@
         copy.wait()
     project(me)
     for step in range(steps):
-        forward(0, step)
+        forward(step)
         if step == steps - 2:
-            send(1)
+
+            @pl.when(outer)
+            def _():
+                w_start(0, 0)
+                hidden_copy.start()
+
+            @pl.when(inner)
+            def _():
+                w_start(0, 2)
+
         project(ring_index(place - 1 - step, shards))
         if step < steps - 1:
             project(ring_index(place + 1 + step, shards))
@@ -268,82 +327,140 @@
             result = jnp.where(mine, mixed / total, result)
         return result.astype(jnp.bfloat16)
 
-    def out_copy(away):
-        peer = lax.rem(me + away, shards)
-        return pltpu.make_async_remote_copy(
-            src_ref=outbox.at[away - 1],
-            dst_ref=attended_ref.at[:, my_columns],
-            send_sem=out_send.at[away - 1],
-            recv_sem=out_recv.at[away - 1],
-            device_id={"seq": peer},
-            device_id_type=MESH,
-        )
-
-    for away in range(1, shards + 1):
-        if away < shards:
-            outbox[away - 1] = attend(lax.rem(me + away, shards))
-            out_copy(away).start()
+    def out_copy(turn, target):
+        return remote(
+            outbox.at[turn],
+            attended_ref.at[:, my_columns],
+            out_send.at[turn],
+            out_recv.at[me],
+            target,
+        )
+
+    turns = steps
+
+    def target_of(turn):
+        return 2 + lax.rem(home - 2 + 1 + turn, turns)
+
+    for turn in range(turns):
+        target = target_of(turn)
+        outbox[turn, :rows, :] = attend(target)
+        outbox[turn, rows:, :] = attend(partner_of(target))
+        if turn < turns - 1:
+            out_copy(turn, target).start()
         else:
-            attended_ref[:, my_columns] = attend(me)
-        if away == 4:
-            forward(1, 0)
-    forward(1, 1)
-    for piece in range(2):
-        b_copy(0, piece).start()
-    for piece in range(2):
-        b_copy(1, piece).start()
-    forward(1, 2)
-    for away in range(1, shards):
-        out_copy(away).wait_recv()
-    kept[0].wait()
-    forward(1, 3)
-    tile = 2 * width
-
-    def joined(full, pair):
-        return jnp.concatenate([full[2 * pair], full[2 * pair + 1]], axis=1)
-
-    for at in range(0, depth, tile):
-        cols = slice(at, at + tile)
-        after[:, cols] = hidden[:, cols].astype(jnp.float32) + jnp.dot(
-            attended_ref[...], joined(full_a_ref, at // tile), preferred_element_type=jnp.float32
-        )
-    conv_rows[0, margin : margin + rows, :] = layer_norm(after[...]).astype(jnp.bfloat16)
-
-    rows_copy = pltpu.make_async_remote_copy(
-        src_ref=conv_rows.at[0, pl.ds(margin, rows), :],
-        dst_ref=conv_rows.at[1, pl.ds(margin, rows), :],
-        send_sem=rows_send,
-        recv_sem=rows_recv,
-        device_id={"seq": partner},
-        device_id_type=MESH,
-    )
-    rows_copy.start()
-
-    def edge_copy(side, slot):
-        owner = lax.rem(me + (1 if side == 0 else shards - 1), shards)
+
+            @pl.when(outer)
+            def _():
+                out_copy(turns - 1, partner).start()
+
+            @pl.when(inner)
+            def _():
+                attended_ref[:, my_columns] = outbox[turns - 1]
+
+        if turn == 2:
+
+            @pl.when(inner)
+            def _():
+                w_wait(0, 0, (3, 4))
+                w_wait(0, 2, (5,))
+
+    b_start(0)
+
+    @pl.when(outer)
+    def _():
+        b_start(1)
+
+    def rows_copy(slot):
+        return remote(
+            conv_rows.at[slot, pl.ds(margin, rows), :],
+            conv_rows.at[1 - slot, pl.ds(margin, rows), :],
+            rows_send.at[slot],
+            rows_recv.at[slot],
+            partner,
+        )
+
+    def edge_copy(slot, side, deep):
+        source = me if slot == 0 else partner
+        owner = lax.rem(source + (1 if side == 0 else shards - 1), shards)
+        is_inner = inner_of(owner)
         first, at = (rows, 0) if side == 0 else (margin, margin + rows)
-        return pltpu.make_async_remote_copy(
-            src_ref=conv_rows.at[0, pl.ds(first, margin), :],
-            dst_ref=conv_rows.at[slot, pl.ds(at, margin), :],
-            send_sem=edge_send.at[side, slot],
-            recv_sem=edge_recv.at[side, slot],
-            device_id={"seq": owner if slot == 0 else partner_of(owner)},
-            device_id_type=MESH,
-        )
-
-    edges = [edge_copy(side, slot) for slot in range(2) for side in range(2)]
-    for copy in edges:
-        copy.start()
-    for piece in range(2):
+        peer = is_inner * owner + (1 - is_inner) * partner_of(owner)
+        where = 1 - is_inner
+        if deep == 1:
+            peer, where = partner_of(peer), is_inner
+        return remote(
+            conv_rows.at[slot, pl.ds(first, margin), :],
+            conv_rows.at[where, pl.ds(at, margin), :],
+            edge_send.at[slot, side, deep],
+            edge_recv.at[where, side],
+            peer,
+        )
+
+    def edge_arrival(slot, side):
+        at = 0 if side == 0 else margin + rows
+        block = conv_rows.at[slot, pl.ds(at, margin), :]
+        return remote(block, block, edge_send.at[0, 0, 0], edge_recv.at[slot, side], partner)
+
+    @pl.when(inner)
+    def _():
+        w_wait(0, 3, (6,))
+        for away in range(1, shards):
+            source = lax.rem(me + away, shards)
+            remote(
+                outbox.at[0],
+                attended_ref.at[:, my_columns],
+                out_send.at[0],
+                out_recv.at[source],
+                source,
+            ).wait_recv()
+        hidden_copy.wait_recv()
+        kept[0].wait()
+
+        def output_part(owner):
+            at = lax.div(owner, 2)
+            cols = pl.ds(pl.multiple_of(at * (2 * width), 128), 2 * width)
+            after[:, cols] = hidden[:, cols].astype(jnp.float32) + jnp.dot(
+                attended_ref[...], full_a_ref[at], preferred_element_type=jnp.float32
+            )
+
+        w_wait(0, 1)
+        output_part(me)
+        w_wait(0, 4)
+        output_part(partner)
+        w_wait(0, 5)
+        output_part(facing)
+        w_wait(0, 6)
+        output_part(partner_of(facing))
+        for slot in (1, 0):
+            block = layer_norm(after[slot * rows : (slot + 1) * rows, :]).astype(jnp.bfloat16)
+            conv_rows[slot, margin : margin + rows, :] = block
+            for side in range(2):
+                for deep in range(2):
+                    edge_copy(slot, side, deep).start()
+            rows_copy(slot).start()
+
+    for piece in b_pieces:
         b_copy(0, piece).wait_recv()
         b_copy(2, piece).start()
-    send(2)
+
+    @pl.when(inner)
+    def _():
+        w_start(1, 1)
+        w_start(1, 2)
+
+    @pl.when(outer)
+    def _():
+        kept[0].wait()
+        w_start(1, 0)
+        for slot in range(2):
+            rows_copy(slot).wait_recv()
+
     kept[1].wait()
-    rows_copy.wait_recv()
-    for copy in edges:
-        copy.wait_recv()
-
-    part = w_b_ref.shape[1]
+    kept[2].wait()
+    for slot in range(2):
+        for side in range(2):
+            edge_arrival(slot, side).wait_recv()
+
     reach = KERNEL // 2
 
     def gate(piece):
@@ -364,95 +481,118 @@
             term = padded[slot, start : start + rows, at : at + 128] * block[offset : offset + 1]
             keep = near[slot, start : start + rows, :] == own
             summed = summed + jnp.where(keep, term, 0.0)
-        if slot == 0:
-            depthwise[:, cols] = summed
-        else:
-            deep_out[:, pl.ds(pl.multiple_of(piece * part + at, 128), 128)] = summed.astype(
-                jnp.bfloat16
-            )
-
-    def deep_copy(order):
+        depthwise[slot * rows : (slot + 1) * rows, cols] = summed
+        deep_cols = pl.ds(pl.multiple_of(piece * part + at, 128), 128)
+        deep_out[slot, :, deep_cols] = summed.astype(jnp.bfloat16)
+
+    def deep_copy(order, slot):
         piece = odd if order == 0 else 1 - odd
         cols = pl.ds(pl.multiple_of(piece * part, 128), part)
-        return pltpu.make_async_remote_copy(
-            src_ref=deep_out.at[:, cols],
-            dst_ref=deep_in.at[:, cols],
-            send_sem=deep_send.at[order],
-            recv_sem=deep_recv.at[order],
-            device_id={"seq": partner},
-            device_id_type=MESH,
+        return remote(
+            deep_out.at[slot, :, cols],
+            deep_in.at[1 - slot, :, cols],
+            deep_send.at[order, slot],
+            deep_recv.at[order, slot],
+            partner,
         )
 
     def convolve(order):
         piece = odd if order == 0 else 1 - odd
         gate(piece)
-        for at in range(0, part, 128):
-            taps_of(piece, 1, at)
-        deep_copy(order).start()
-        for at in range(0, part, 128):
-            taps_of(piece, 0, at)
+        for slot in range(2):
+            for at in range(0, part, 128):
+                taps_of(piece, slot, at)
+
+            @pl.when(outer)
+            def _():
+                deep_copy(order, slot).start()
 
     convolve(0)
-    forward(2, 0)
+
+    @pl.when(inner)
+    def _():
+        w_wait(1, 0, (3, 4))
+        w_wait(1, 2, (5,))
+
     for kind in (1, 2):
-        for piece in range(2):
+        for piece in b_pieces:
             b_copy(kind, piece).wait_recv()
     convolve(1)
-    forward(2, 1)
-    for order in range(2):
-        deep_copy(order).wait_recv()
-    other = pl.ds(pl.multiple_of((1 - half) * (2 * part), 128), 2 * part)
-    depthwise[:, other] = deep_in[...].astype(jnp.float32)
-    conv_act = layer_norm(depthwise[...])
-    conv_act = (conv_act * jax.nn.sigmoid(conv_act)).astype(jnp.bfloat16)
-
-    def leave(piece, owner):
-        cols = pl.ds(pl.multiple_of(owner * width, 128), width)
-        return pltpu.make_async_remote_copy(
-            src_ref=leaving.at[:, cols],
-            dst_ref=handed_ref.at[:, cols],
-            send_sem=leave_send.at[piece],
-            recv_sem=leave_recv.at[piece],
-            device_id={"phase": phase_next},
-            device_id_type=MESH,
-        )
-
-    sent = []
-
-    def finish(owner):
-        cols = pl.ds(pl.multiple_of(owner * width, 128), width)
-        leaving[:, cols] = (
-            after[:, cols]
-            + jnp.dot(conv_act, full_c_ref[owner], preferred_element_type=jnp.float32)
-        ).astype(jnp.bfloat16)
-        copy = leave(len(sent), owner)
-        copy.start()
-        sent.append(copy)
-
-    kept[2].wait()
-    finish(me)
+
+    def leave(turn, slot, owner):
+        cols = pl.ds(pl.multiple_of(lax.div(owner, 2) * (2 * width), 128), 2 * width)
+        return remote(
+            leaving.at[pl.ds(slot * rows, rows), cols],
+            handed_ref.at[:, cols],
+            leave_send.at[turn, slot],
+            leave_recv.at[turn],
+            me if slot == 0 else partner,
+            phase_next,
+        )
+
+    ends = (me, partner, facing, partner_of(facing))
+
+    @pl.when(inner)
+    def _():
+        w_wait(1, 3, (6,))
+        for order in range(2):
+            for slot in range(2):
+                deep_copy(order, slot).wait_recv()
+        other = pl.ds(pl.multiple_of((1 - half) * (2 * part), 128), 2 * part)
+        for slot in range(2):
+            at = slice(slot * rows, (slot + 1) * rows)
+            depthwise[at, other] = deep_in[slot].astype(jnp.float32)
+            block = layer_norm(depthwise[at, :])
+            conv_act[at, :] = (block * jax.nn.sigmoid(block)).astype(jnp.bfloat16)
+        for turn, owner in enumerate(ends):
+            for kind in ((1,), (4,), (5,), (6,))[turn]:
+                w_wait(1, kind)
+            at = lax.div(owner, 2)
+            cols = pl.ds(pl.multiple_of(at * (2 * width), 128), 2 * width)
+            leaving[:, cols] = (
+                after[:, cols]
+                + jnp.dot(conv_act[...], full_c_ref[at], preferred_element_type=jnp.float32)
+            ).astype(jnp.bfloat16)
+            for slot in (1, 0):
+                leave(turn, slot, owner).start()
+
     for step in range(steps):
-        if step >= 2:
-            forward(2, step)
-        finish(ring_index(place - 1 - step, shards))
-        if step < steps - 1:
-            finish(ring_index(place + 1 + step, shards))
-    for away in range(1, shards):
-        out_copy(away).wait_send()
-    rows_copy.wait_send()
-    for copy in edges:
-        copy.wait_send()
-    for order in range(2):
-        deep_copy(order).wait_send()
+        for way, piece in hops(step):
+            hop(step, way, piece).wait_send()
+    for turn in range(turns - 1):
+        out_copy(turn, target_of(turn)).wait_send()
     for kind in range(3):
-        for piece in range(2):
+        for piece in b_pieces:
             b_copy(kind, piece).wait_send()
-    for load in range(3):
-        for step in range(steps):
-            for way, piece in hops(step):
-                hop(load, step, way, piece).wait_send()
-    for copy in sent:
-        copy.wait()
+
+    @pl.when(outer)
+    def _():
+        out_copy(turns - 1, partner).wait_send()
+        hidden_copy.wait_send()
+        for load in range(2):
+            for piece in wholes:
+                w_copy(load, 0, piece).wait_send()
+        for order in range(2):
+            for slot in range(2):
+                deep_copy(order, slot).wait_send()
+
+    @pl.when(inner)
+    def _():
+        for load in range(2):
+            for kind in range(1, 7):
+                for piece in wholes:
+                    w_copy(load, kind, piece).wait_send()
+        for slot in range(2):
+            rows_copy(slot).wait_send()
+            for side in range(2):
+                for deep in range(2):
+                    edge_copy(slot, side, deep).wait_send()
+        for turn, owner in enumerate(ends):
+            for slot in range(2):
+                leave(turn, slot, owner).wait_send()
+
+    for turn, owner in enumerate(ends):
+        leave(turn, 0, owner).wait_recv()
 
 
 def block_call(shards, hidden, lengths, taps, weights):
@@ -473,42 +613,47 @@
         in_specs=[smem, anywhere, vmem] + [anywhere] * 6,
         out_specs=vmem,
         scratch_shapes=[
-            pltpu.VMEM((rows, depth), bf16),
+            pltpu.VMEM((2 * rows, depth), bf16),
             pltpu.VMEM((depth, 3 * width), bf16),
-            pltpu.VMEM((shards, depth, width), bf16),
+            pltpu.VMEM((shards // 2, depth, 2 * width), bf16),
             pltpu.VMEM((shards // 2, depth, part), bf16),
-            pltpu.VMEM((shards, depth, width), bf16),
-            pltpu.VMEM((rows, depth), bf16),
-            pltpu.VMEM((rows, depth), f32),
+            pltpu.VMEM((shards // 2, depth, 2 * width), bf16),
+            pltpu.VMEM((2 * rows, depth), bf16),
+            pltpu.VMEM((2 * rows, depth), f32),
             pltpu.VMEM((2, rows + 2 * margin, depth), bf16),
             pltpu.VMEM((2, rows + 2 * margin, 128), jnp.int32),
             pltpu.VMEM(taps.shape, f32),
             pltpu.VMEM((2, rows + 2 * margin, part), f32),
-            pltpu.VMEM((rows, depth), f32),
-            pltpu.VMEM((rows, depth // 2), bf16),
-            pltpu.VMEM((rows, depth // 2), bf16),
-            pltpu.VMEM((rows, depth), bf16),
+            pltpu.VMEM((2 * rows, depth), f32),
+            pltpu.VMEM((2, rows, depth // 2), bf16),
+            pltpu.VMEM((2, rows, depth // 2), bf16),
+            pltpu.VMEM((2 * rows, depth), bf16),
+            pltpu.VMEM((2 * rows, depth), bf16),
             pltpu.VMEM((total, depth), bf16),
             pltpu.VMEM((total, width), bf16),
             pltpu.VMEM((total, width), bf16),
             pltpu.VMEM((total, width), bf16),
-            pltpu.VMEM((shards - 1, rows, width), bf16),
-            dma((3 * steps * 2, 2)),
-            dma((3 * steps * 2, 2)),
+            pltpu.VMEM((steps, 2 * rows, width), bf16),
+            dma((2 * steps, 2)),
+            dma((2 * steps, 2)),
             dma((3,)),
-            dma((shards - 1,)),
-            dma((shards - 1,)),
+            dma((steps,)),
+            dma((shards,)),
             dma((4,)),
-            dma((3, 2)),
-            dma((3, 2)),
+            dma((2, 7, 2)),
+            dma((2, 7, 2)),
+            dma((3, 4)),
+            dma((3, 4)),
             dma,
             dma,
+            dma((2,)),
+            dma((2,)),
+            dma((2, 2, 2)),
             dma((2, 2)),
             dma((2, 2)),
-            dma((2,)),
-            dma((2,)),
-            dma((shards,)),
-            dma((shards,)),
+            dma((2, 2)),
+            dma((steps, 2)),
+            dma((steps,)),
         ],
         compiler_params=pltpu.CompilerParams(
             collective_id=0, has_side_effects=True, vmem_limit_bytes=56 * 1024 * 1024

time: 122 us -> 112 us (0.918)
  Pallas kernels: 120 us -> 110 us
    pallas_call x1, Pallas kernels: 120 us -> 110 us  [block_call(): pl.pallas_call(functools.partial(block_kernel, shards, depth // HEADS), o...]
where the time goes in v2:
time: 112 us
  Pallas kernels  110 us (98%)
  local copies, waits for them, and re-layouts  1.72 us (2%)
    pallas_call x1, Pallas kernels, block_call(): pl.pallas_call(functools.partial(block_kernel, shards, depth // HEADS), o...  110 us

profile of v2, /device:TPU:1, one launch (start us, length us, event | category | flops | bytes accessed | tf_op | source)
XLA Modules:
  0.0 111.9 jit_solution(8785039668929658969)
XLA Ops:
  0.0 110.2 %shard_map.91 = bf16[160,1024]{1,0:T(8,128)(2,1)} custom-call(s32[8]{0:T(128)} %bitcast.19, bf16[160,1024]{1,0:T(8,128)(2,1)} %bitcast.12, bf16[31,1024]{1,0:T(8,128)(2,1)} %bitcast.18, bf16[1024,128]{1,0:T(8,128)(2,1)} %bitcast.13, bf16[1024,128]{1,0:T(8,128)(2,1)} %bitcast.14, bf16[1024,128]{1,0:T(8,128)(2,1)} %bitcast.15, bf16[1024,128]{1,0:T(8,128)(2,1)} %bitcast.16, ...), custom_call_target="tpu_custom_call" | custom-call | tf_op jit(solution)/shard_map/pallas_call | solution.py:610
  110.2 1.7 %copy.11 = bf16[1,160,1024]{2,1,0:T(8,128)(2,1)} copy(bf16[1,160,1024]{2,1,0:T(8,128)(2,1)} %bitcast.10) | data formatting | bytes 655360

commit v3 on v2

--- a/solution.py
+++ b/solution.py
@@ -84,9 +84,7 @@
     depthwise,
     deep_out,
     deep_in,
-    conv_act,
     leaving,
-    normed,
     query,
     keys,
     values,
@@ -99,10 +97,6 @@
     in_sem,
     w_send,
     w_recv,
-    b_send,
-    b_recv,
-    hidden_send,
-    hidden_recv,
     rows_send,
     rows_recv,
     edge_send,
@@ -116,7 +110,9 @@
     depth = frames_ref.shape[1]
     width = query_ref.shape[1]
     part = w_b_ref.shape[1]
-    loads_in = [pltpu.make_async_copy(frames_ref, hidden.at[pl.ds(0, rows), :], in_sem.at[3])]
+    me = lax.axis_index("seq")
+    own_rows = pl.ds(pl.multiple_of(me * rows, rows), rows)
+    loads_in = [pltpu.make_async_copy(frames_ref, hidden.at[own_rows, :], in_sem.at[3])]
     for i, ref in enumerate((query_ref, key_ref, value_ref)):
         loads_in.append(
             pltpu.make_async_copy(ref, qkv.at[:, pl.ds(i * width, width)], in_sem.at[i])
@@ -124,7 +120,6 @@
     for copy in loads_in:
         copy.start()
     steps = shards // 2
-    me = lax.axis_index("seq")
     odd = lax.rem(me, 2)
     place = (1 - odd) * lax.div(me, 2) + odd * (shards - 1 - lax.div(me, 2))
     right, left = ring_index(place + 1, shards), ring_index(place - 1, shards)
@@ -138,7 +133,6 @@
         return lax.rem(lax.div(lax.div(owner, 2) + 1, 2), 2)
 
     beside = me + 1 - 2 * odd
-    across = me + 4 - 8 * upper
     facing = me + 2 - 4 * upper
     partner = partner_of(me)
     inner = inner_of(me) == 1
@@ -160,8 +154,6 @@
             )
 
     loads_in[0].wait()
-    own_rows = pl.ds(pl.multiple_of(me * rows, rows), rows)
-    normed[own_rows, :] = layer_norm(hidden[:rows, :].astype(jnp.float32)).astype(jnp.bfloat16)
     pl.semaphore_wait(barrier, shards + 3)
 
     def remote(source, target, sent, got, peer, onward=None):
@@ -178,7 +170,7 @@
     def hop(step, way, piece):
         owner = ring_index(place - step if way == 0 else place + step, shards)
         size = rows // 2
-        block = normed.at[pl.ds(pl.multiple_of(owner * rows + piece * size, 16), size), :]
+        block = hidden.at[pl.ds(pl.multiple_of(owner * rows + piece * size, 16), size), :]
         at = step * 2 + way
         peer = right if way == 0 else left
         return remote(block, block, send_sem.at[at, piece], recv_sem.at[at, piece], peer)
@@ -196,26 +188,29 @@
 
     def project(owner):
         at = pl.ds(pl.multiple_of(owner * rows, rows), rows)
-        block = normed[at, :]
+        block = layer_norm(hidden[at, :].astype(jnp.float32)).astype(jnp.bfloat16)
         both = jnp.dot(block, qkv[...], preferred_element_type=jnp.float32).astype(jnp.bfloat16)
         query[at, :] = both[:, :width] * jnp.bfloat16(1.0 / math.sqrt(head_size))
         keys[at, :] = both[:, width : 2 * width]
         values[at, :] = both[:, 2 * width :]
 
-    fulls = ((w_a_ref, full_a_ref), (w_c_ref, full_c_ref))
+    fulls = ((w_a_ref, full_a_ref), (w_c_ref, full_c_ref), (w_b_ref, half_b_ref))
     wholes = range(2)
 
-    def chunk(full, owner, first, size):
+    def chunk(load, owner, first, size):
+        full = fulls[load][1]
+        if load == 2:
+            return full.at[lax.div(owner, 2), pl.ds(first, size), :]
         cols = pl.ds(pl.multiple_of(lax.rem(owner, 2) * width, 128), width)
         return full.at[lax.div(owner, 2), pl.ds(first, size), cols]
 
     def w_copy(load, kind, piece):
-        own, full = fulls[load]
+        own = fulls[load][0]
         size = depth // 2
-        owner = (me, me, me, partner, partner, facing, partner_of(facing))[kind]
-        peer = (partner, beside, facing, facing, beside, beside, beside)[kind]
-        target = chunk(full, owner, piece * size, size)
-        source = own.at[pl.ds(piece * size, size), :] if kind < 3 else target
+        owner = (me, me, me, partner, beside, facing, partner_of(facing), me)[kind]
+        peer = (partner, beside, facing, facing, partner, beside, beside, beside)[kind]
+        target = chunk(load, owner, piece * size, size)
+        source = own.at[pl.ds(piece * size, size), :] if kind in (0, 1, 2, 7) else target
         return remote(
             source, target, w_send.at[load, kind, piece], w_recv.at[load, kind, piece], peer
         )
@@ -230,54 +225,33 @@
             for more in then:
                 w_copy(load, more, piece).start()
 
-    def b_slot(owner):
-        return lax.div(owner, 4) * 2 + lax.rem(owner, 2)
-
-    b_pieces = range(4)
-
-    def b_copy(kind, piece):
-        size = depth // len(b_pieces)
-        at = pl.ds(piece * size, size)
-        target = half_b_ref.at[b_slot(across if kind == 2 else me), at, :]
-        source = target if kind == 2 else w_b_ref.at[at, :]
-        peer = across if kind == 0 else beside
-        return remote(source, target, b_send.at[kind, piece], b_recv.at[kind, piece], peer)
-
-    def b_start(kind):
-        for piece in b_pieces:
-            b_copy(kind, piece).start()
-
     for way, piece in hops(0):
         hop(0, way, piece).start()
 
     @pl.when(inner)
     def _():
         w_start(0, 1)
-        b_start(1)
+        w_start(1, 1)
 
     kept = [
-        pltpu.make_async_copy(w_a_ref, chunk(full_a_ref, me, 0, depth), own_sem.at[0]),
-        pltpu.make_async_copy(w_b_ref, half_b_ref.at[b_slot(me)], own_sem.at[1]),
-        pltpu.make_async_copy(w_c_ref, chunk(full_c_ref, me, 0, depth), own_sem.at[2]),
+        pltpu.make_async_copy(fulls[load][0], chunk(load, me, 0, depth), own_sem.at[load])
+        for load in range(3)
     ]
     for copy in kept:
         copy.start()
-    hidden_copy = remote(
-        hidden.at[pl.ds(0, rows), :],
-        hidden.at[pl.ds(rows, rows), :],
-        hidden_send,
-        hidden_recv,
-        partner,
-    )
-
     bounds = [lengths_ref[0]]
     for utt in range(1, lengths_ref.shape[0]):
         bounds.append(bounds[-1] + lengths_ref[utt])
     seg_col = segment_of(lax.broadcasted_iota(jnp.int32, (1, rows * shards), 1), bounds)
-    margin = (near.shape[1] - rows) // 2
-    for slot, owner in enumerate((me, partner)):
-        positions = lax.broadcasted_iota(jnp.int32, near.shape[1:], 0) + (owner * rows - margin)
-        near[slot] = jnp.where(positions >= 0, segment_of(positions, bounds), -1)
+    margin = 16
+    span = rows * steps
+    first_row = upper * span
+    for shift in range(near.shape[0]):
+        positions = lax.broadcasted_iota(jnp.int32, near.shape[1:], 0)
+        positions = positions + (first_row + shift - KERNEL // 2)
+        near[shift] = jnp.where(positions >= 0, segment_of(positions, bounds), -1)
+    outside = pl.multiple_of(upper * (span + margin), 16)
+    conv_rows[pl.ds(outside, margin), :] = jnp.zeros((margin, depth), jnp.bfloat16)
     taps[...] = taps_ref[...].astype(jnp.float32)
 
     for copy in loads_in[1:]:
@@ -290,7 +264,7 @@
             @pl.when(outer)
             def _():
                 w_start(0, 0)
-                hidden_copy.start()
+                w_start(0, 7)
 
             @pl.when(inner)
             def _():
@@ -361,45 +335,115 @@
 
             @pl.when(inner)
             def _():
-                w_wait(0, 0, (3, 4))
+                w_wait(0, 0, (3,))
                 w_wait(0, 2, (5,))
-
-    b_start(0)
 
     @pl.when(outer)
     def _():
-        b_start(1)
+        w_wait(0, 7, (4,))
+        w_start(2, 0)
+        for piece in wholes:
+            w_copy(2, 0, piece).wait_send()
+        w_start(1, 0)
+        w_start(1, 7)
+        w_wait(1, 7, (4,))
+
+    @pl.when(inner)
+    def _():
+        w_start(2, 2)
+
+    slot_rows = [
+        pl.multiple_of((owner - 4 * upper) * rows, 16) for owner in (me, partner)
+    ]
+    other_rows = [
+        pl.multiple_of((owner - 4 * upper) * rows, 16)
+        for owner in (beside, partner_of(beside))
+    ]
 
     def rows_copy(slot):
+        block = conv_rows.at[pl.ds(pl.multiple_of(slot_rows[slot] + margin, 16), rows), :]
+        return remote(block, block, rows_send.at[slot], rows_recv.at[slot], beside)
+
+    def edge_copy(turn):
+        source = pl.multiple_of((1 - upper) * span + upper * margin, 16)
+        target = pl.multiple_of(upper * (span + margin), 16)
         return remote(
-            conv_rows.at[slot, pl.ds(margin, rows), :],
-            conv_rows.at[1 - slot, pl.ds(margin, rows), :],
-            rows_send.at[slot],
-            rows_recv.at[slot],
-            partner,
-        )
-
-    def edge_copy(slot, side, deep):
-        source = me if slot == 0 else partner
-        owner = lax.rem(source + (1 if side == 0 else shards - 1), shards)
-        is_inner = inner_of(owner)
-        first, at = (rows, 0) if side == 0 else (margin, margin + rows)
-        peer = is_inner * owner + (1 - is_inner) * partner_of(owner)
-        where = 1 - is_inner
-        if deep == 1:
-            peer, where = partner_of(peer), is_inner
+            conv_rows.at[pl.ds(source, margin), :],
+            conv_rows.at[pl.ds(target, margin), :],
+            edge_send.at[turn],
+            edge_recv,
+            facing if turn == 0 else facing + 1 - 2 * odd,
+        )
+
+    lends = inner & (odd + upper == 1)
+    reach = KERNEL // 2
+
+    def gate(piece):
+        for at in range(0, span + 2 * margin, (span + 2 * margin) // 2):
+            block = slice(at, at + (span + 2 * margin) // 2)
+            value = jnp.dot(
+                conv_rows[block, :], half_b_ref[piece], preferred_element_type=jnp.float32
+            )
+            gates = jnp.dot(
+                conv_rows[block, :], half_b_ref[2 + piece], preferred_element_type=jnp.float32
+            )
+            glu = (value * jax.nn.sigmoid(gates)).astype(jnp.bfloat16)
+            padded[block, :] = glu.astype(jnp.float32)
+
+    def columns_of(piece, side, at):
+        return pl.ds(pl.multiple_of(piece * (2 * part) + side * part + at, 128), 128)
+
+    def taps_of(piece, at):
+        cols = columns_of(piece, odd, at)
+        block = taps[:, cols]
+        size = rows // 2
+        for first in range(0, span, size):
+            own = near[reach % 8, first + reach // 8 * 8 : first + reach // 8 * 8 + size, :]
+            summed = jnp.zeros((size, 128), jnp.float32)
+            for shift in range(8):
+                start = first + margin - reach + shift
+                ahead = padded[start : start + size + 24, at : at + 128]
+                for skip in range(0, 32, 8):
+                    offset = skip + shift
+                    if offset < KERNEL:
+                        term = ahead[skip : skip + size] * block[offset : offset + 1]
+                        keep = near[shift, first + skip : first + skip + size, :] == own
+                        summed = summed + jnp.where(keep, term, 0.0)
+            depthwise[first : first + size, cols] = summed
+
+    def deep_copy(order, at):
+        turn = order * 2 + at // 128
         return remote(
-            conv_rows.at[slot, pl.ds(first, margin), :],
-            conv_rows.at[where, pl.ds(at, margin), :],
-            edge_send.at[slot, side, deep],
-            edge_recv.at[where, side],
-            peer,
-        )
-
-    def edge_arrival(slot, side):
-        at = 0 if side == 0 else margin + rows
-        block = conv_rows.at[slot, pl.ds(at, margin), :]
-        return remote(block, block, edge_send.at[0, 0, 0], edge_recv.at[slot, side], partner)
+            deep_out.at[turn], deep_in.at[turn], deep_send.at[turn], deep_recv.at[turn], beside
+        )
+
+    def piece_of(order):
+        return upper if order == 0 else 1 - upper
+
+    def convolve(order):
+        piece = piece_of(order)
+        gate(piece)
+        for at in range(0, part, 128):
+            taps_of(piece, at)
+            cols = columns_of(piece, odd, at)
+            for slot in range(2):
+                deep_out[order * 2 + at // 128, slot * rows : (slot + 1) * rows, :] = depthwise[
+                    pl.ds(other_rows[slot], rows), cols
+                ].astype(jnp.bfloat16)
+            deep_copy(order, at).start()
+
+    def leave(turn, slot, owner):
+        cols = pl.ds(pl.multiple_of(lax.div(owner, 2) * (2 * width), 128), 2 * width)
+        return remote(
+            leaving.at[pl.ds(slot * rows, rows), cols],
+            handed_ref.at[:, cols],
+            leave_send.at[turn, slot],
+            leave_recv.at[turn],
+            me if slot == 0 else partner,
+            phase_next,
+        )
+
+    ends = (me, partner, facing, partner_of(facing))
 
     @pl.when(inner)
     def _():
@@ -413,15 +457,16 @@
                 out_recv.at[source],
                 source,
             ).wait_recv()
-        hidden_copy.wait_recv()
         kept[0].wait()
 
         def output_part(owner):
             at = lax.div(owner, 2)
             cols = pl.ds(pl.multiple_of(at * (2 * width), 128), 2 * width)
-            after[:, cols] = hidden[:, cols].astype(jnp.float32) + jnp.dot(
-                attended_ref[...], full_a_ref[at], preferred_element_type=jnp.float32
-            )
+            mixed = jnp.dot(attended_ref[...], full_a_ref[at], preferred_element_type=jnp.float32)
+            for slot, source in enumerate((me, partner)):
+                block = slice(slot * rows, (slot + 1) * rows)
+                first = pl.ds(pl.multiple_of(source * rows, rows), rows)
+                after[block, cols] = hidden[first, cols].astype(jnp.float32) + mixed[block]
 
         w_wait(0, 1)
         output_part(me)
@@ -431,129 +476,53 @@
         output_part(facing)
         w_wait(0, 6)
         output_part(partner_of(facing))
-        for slot in (1, 0):
+        for slot in (0, 1):
             block = layer_norm(after[slot * rows : (slot + 1) * rows, :]).astype(jnp.bfloat16)
-            conv_rows[slot, margin : margin + rows, :] = block
-            for side in range(2):
-                for deep in range(2):
-                    edge_copy(slot, side, deep).start()
+            at = pl.ds(pl.multiple_of(slot_rows[slot] + margin, 16), rows)
+            conv_rows[at, :] = block
+            if slot == 0:
+
+                @pl.when(lends)
+                def _():
+                    for turn in range(2):
+                        edge_copy(turn).start()
+
             rows_copy(slot).start()
-
-    for piece in b_pieces:
-        b_copy(0, piece).wait_recv()
-        b_copy(2, piece).start()
-
-    @pl.when(inner)
-    def _():
-        w_start(1, 1)
+        w_wait(2, 0, (3,))
         w_start(1, 2)
-
-    @pl.when(outer)
-    def _():
-        kept[0].wait()
-        w_start(1, 0)
+        w_wait(1, 0, (3,))
+        kept[2].wait()
+        w_wait(2, 2)
+        edge_copy(0).wait_recv()
         for slot in range(2):
             rows_copy(slot).wait_recv()
-
-    kept[1].wait()
-    kept[2].wait()
-    for slot in range(2):
-        for side in range(2):
-            edge_arrival(slot, side).wait_recv()
-
-    reach = KERNEL // 2
-
-    def gate(piece):
-        for slot in range(2):
-            block = conv_rows[slot]
-            value = jnp.dot(block, half_b_ref[piece], preferred_element_type=jnp.float32)
-            gates = jnp.dot(block, half_b_ref[2 + piece], preferred_element_type=jnp.float32)
-            glu = (value * jax.nn.sigmoid(gates)).astype(jnp.bfloat16)
-            padded[slot] = glu.astype(jnp.float32)
-
-    def taps_of(piece, slot, at):
-        cols = pl.ds(pl.multiple_of(half * (2 * part) + piece * part + at, 128), 128)
-        block = taps[:, cols]
-        own = near[slot, margin : margin + rows, :]
-        summed = jnp.zeros((rows, 128), jnp.float32)
-        for offset in range(KERNEL):
-            start = margin - reach + offset
-            term = padded[slot, start : start + rows, at : at + 128] * block[offset : offset + 1]
-            keep = near[slot, start : start + rows, :] == own
-            summed = summed + jnp.where(keep, term, 0.0)
-        depthwise[slot * rows : (slot + 1) * rows, cols] = summed
-        deep_cols = pl.ds(pl.multiple_of(piece * part + at, 128), 128)
-        deep_out[slot, :, deep_cols] = summed.astype(jnp.bfloat16)
-
-    def deep_copy(order, slot):
-        piece = odd if order == 0 else 1 - odd
-        cols = pl.ds(pl.multiple_of(piece * part, 128), part)
-        return remote(
-            deep_out.at[slot, :, cols],
-            deep_in.at[1 - slot, :, cols],
-            deep_send.at[order, slot],
-            deep_recv.at[order, slot],
-            partner,
-        )
-
-    def convolve(order):
-        piece = odd if order == 0 else 1 - odd
-        gate(piece)
-        for slot in range(2):
+        w_wait(1, 2, (5,))
+        convolve(0)
+        w_wait(1, 3, (6,))
+        w_wait(2, 3)
+        convolve(1)
+        for order in range(2):
             for at in range(0, part, 128):
-                taps_of(piece, slot, at)
-
-            @pl.when(outer)
-            def _():
-                deep_copy(order, slot).start()
-
-    convolve(0)
-
-    @pl.when(inner)
-    def _():
-        w_wait(1, 0, (3, 4))
-        w_wait(1, 2, (5,))
-
-    for kind in (1, 2):
-        for piece in b_pieces:
-            b_copy(kind, piece).wait_recv()
-    convolve(1)
-
-    def leave(turn, slot, owner):
-        cols = pl.ds(pl.multiple_of(lax.div(owner, 2) * (2 * width), 128), 2 * width)
-        return remote(
-            leaving.at[pl.ds(slot * rows, rows), cols],
-            handed_ref.at[:, cols],
-            leave_send.at[turn, slot],
-            leave_recv.at[turn],
-            me if slot == 0 else partner,
-            phase_next,
-        )
-
-    ends = (me, partner, facing, partner_of(facing))
-
-    @pl.when(inner)
-    def _():
-        w_wait(1, 3, (6,))
-        for order in range(2):
-            for slot in range(2):
-                deep_copy(order, slot).wait_recv()
-        other = pl.ds(pl.multiple_of((1 - half) * (2 * part), 128), 2 * part)
-        for slot in range(2):
-            at = slice(slot * rows, (slot + 1) * rows)
-            depthwise[at, other] = deep_in[slot].astype(jnp.float32)
-            block = layer_norm(depthwise[at, :])
-            conv_act[at, :] = (block * jax.nn.sigmoid(block)).astype(jnp.bfloat16)
-        for turn, owner in enumerate(ends):
-            for kind in ((1,), (4,), (5,), (6,))[turn]:
-                w_wait(1, kind)
-            at = lax.div(owner, 2)
-            cols = pl.ds(pl.multiple_of(at * (2 * width), 128), 2 * width)
-            leaving[:, cols] = (
-                after[:, cols]
-                + jnp.dot(conv_act[...], full_c_ref[at], preferred_element_type=jnp.float32)
-            ).astype(jnp.bfloat16)
-            for slot in (1, 0):
+                deep_copy(order, at).wait_recv()
+                cols = columns_of(piece_of(order), 1 - odd, at)
+                for slot in range(2):
+                    depthwise[pl.ds(slot_rows[slot], rows), cols] = deep_in[
+                        order * 2 + at // 128, slot * rows : (slot + 1) * rows, :
+                    ].astype(jnp.float32)
+        kept[1].wait()
+        for slot in (1, 0):
+            block = layer_norm(depthwise[pl.ds(slot_rows[slot], rows), :])
+            act = (block * jax.nn.sigmoid(block)).astype(jnp.bfloat16)
+            at_rows = slice(slot * rows, (slot + 1) * rows)
+            for turn, owner in enumerate(ends):
+                if slot == 1:
+                    w_wait(1, (1, 4, 5, 6)[turn])
+                at = lax.div(owner, 2)
+                cols = pl.ds(pl.multiple_of(at * (2 * width), 128), 2 * width)
+                leaving[at_rows, cols] = (
+                    after[at_rows, cols]
+                    + jnp.dot(act, full_c_ref[at], preferred_element_type=jnp.float32)
+                ).astype(jnp.bfloat16)
                 leave(turn, slot, owner).start()
 
     for step in range(steps):
@@ -561,35 +530,36 @@
             hop(step, way, piece).wait_send()
     for turn in range(turns - 1):
         out_copy(turn, target_of(turn)).wait_send()
-    for kind in range(3):
-        for piece in b_pieces:
-            b_copy(kind, piece).wait_send()
 
     @pl.when(outer)
     def _():
+        for copy in kept:
+            copy.wait()
         out_copy(turns - 1, partner).wait_send()
-        hidden_copy.wait_send()
-        for load in range(2):
-            for piece in wholes:
-                w_copy(load, 0, piece).wait_send()
-        for order in range(2):
-            for slot in range(2):
-                deep_copy(order, slot).wait_send()
+        for load, kinds in ((0, (0, 4, 7)), (1, (0, 4, 7))):
+            for kind in kinds:
+                for piece in wholes:
+                    w_copy(load, kind, piece).wait_send()
 
     @pl.when(inner)
     def _():
-        for load in range(2):
-            for kind in range(1, 7):
+        for load, kinds in ((0, (1, 2, 3, 5, 6)), (1, (1, 2, 3, 5, 6)), (2, (2, 3))):
+            for kind in kinds:
                 for piece in wholes:
                     w_copy(load, kind, piece).wait_send()
         for slot in range(2):
             rows_copy(slot).wait_send()
-            for side in range(2):
-                for deep in range(2):
-                    edge_copy(slot, side, deep).wait_send()
+        for order in range(2):
+            for at in range(0, part, 128):
+                deep_copy(order, at).wait_send()
         for turn, owner in enumerate(ends):
             for slot in range(2):
                 leave(turn, slot, owner).wait_send()
+
+    @pl.when(lends)
+    def _():
+        for turn in range(2):
+            edge_copy(turn).wait_send()
 
     for turn, owner in enumerate(ends):
         leave(turn, 0, owner).wait_recv()
@@ -613,23 +583,21 @@
         in_specs=[smem, anywhere, vmem] + [anywhere] * 6,
         out_specs=vmem,
         scratch_shapes=[
-            pltpu.VMEM((2 * rows, depth), bf16),
+            pltpu.VMEM((total, depth), bf16),
             pltpu.VMEM((depth, 3 * width), bf16),
             pltpu.VMEM((shards // 2, depth, 2 * width), bf16),
             pltpu.VMEM((shards // 2, depth, part), bf16),
             pltpu.VMEM((shards // 2, depth, 2 * width), bf16),
             pltpu.VMEM((2 * rows, depth), bf16),
             pltpu.VMEM((2 * rows, depth), f32),
-            pltpu.VMEM((2, rows + 2 * margin, depth), bf16),
-            pltpu.VMEM((2, rows + 2 * margin, 128), jnp.int32),
+            pltpu.VMEM((total // 2 + 2 * margin, depth), bf16),
+            pltpu.VMEM((8, total // 2 + 24, 128), jnp.int32),
             pltpu.VMEM(taps.shape, f32),
-            pltpu.VMEM((2, rows + 2 * margin, part), f32),
-            pltpu.VMEM((2 * rows, depth), f32),
-            pltpu.VMEM((2, rows, depth // 2), bf16),
-            pltpu.VMEM((2, rows, depth // 2), bf16),
+            pltpu.VMEM((total // 2 + 2 * margin, part), f32),
+            pltpu.VMEM((total // 2, depth), f32),
+            pltpu.VMEM((4, 2 * rows, 128), bf16),
+            pltpu.VMEM((4, 2 * rows, 128), bf16),
             pltpu.VMEM((2 * rows, depth), bf16),
-            pltpu.VMEM((2 * rows, depth), bf16),
-            pltpu.VMEM((total, depth), bf16),
             pltpu.VMEM((total, width), bf16),
             pltpu.VMEM((total, width), bf16),
             pltpu.VMEM((total, width), bf16),
@@ -640,18 +608,14 @@
             dma((steps,)),
             dma((shards,)),
             dma((4,)),
-            dma((2, 7, 2)),
-            dma((2, 7, 2)),
-            dma((3, 4)),
-            dma((3, 4)),
-            dma,
-            dma,
+            dma((3, 8, 2)),
+            dma((3, 8, 2)),
             dma((2,)),
             dma((2,)),
-            dma((2, 2, 2)),
-            dma((2, 2)),
-            dma((2, 2)),
-            dma((2, 2)),
+            dma((2,)),
+            dma,
+            dma((4,)),
+            dma((4,)),
             dma((steps, 2)),
             dma((steps,)),
         ],

time: 112 us -> 111 us (level); the launches traced: 112 us -> 110 us
  Pallas kernels: 110 us -> 108 us
    pallas_call x1, Pallas kernels: 110 us -> 108 us  [block_call(): pl.pallas_call(functools.partial(block_kernel, shards, depth // HEADS), o...]
where the time goes in v3:
time: 111 us; the launch traced here: 110 us
  Pallas kernels  108 us (97%)
  local copies, waits for them, and re-layouts  1.72 us (2%)
    pallas_call x1, Pallas kernels, block_call(): pl.pallas_call(functools.partial(block_kernel, shards, depth // HEADS), o...  108 us

profile of v3, /device:TPU:1, one launch (start us, length us, event | category | flops | bytes accessed | tf_op | source)
XLA Modules:
  0.0 109.6 jit_solution(16215576827469849731)
XLA Ops:
  0.0 107.9 %shard_map.91 = bf16[160,1024]{1,0:T(8,128)(2,1)} custom-call(s32[8]{0:T(128)} %bitcast.19, bf16[160,1024]{1,0:T(8,128)(2,1)} %bitcast.12, bf16[31,1024]{1,0:T(8,128)(2,1)} %bitcast.18, bf16[1024,128]{1,0:T(8,128)(2,1)} %bitcast.13, bf16[1024,128]{1,0:T(8,128)(2,1)} %bitcast.14, bf16[1024,128]{1,0:T(8,128)(2,1)} %bitcast.15, bf16[1024,128]{1,0:T(8,128)(2,1)} %bitcast.16, ...), custom_call_target="tpu_custom_call" | custom-call | tf_op jit(solution)/shard_map/pallas_call | solution.py:580
  107.9 1.7 %copy.11 = bf16[1,160,1024]{2,1,0:T(8,128)(2,1)} copy(bf16[1,160,1024]{2,1,0:T(8,128)(2,1)} %bitcast.10) | data formatting | bytes 655360

commit v4 on v3

--- a/solution.py
+++ b/solution.py
@@ -489,15 +489,15 @@
 
             rows_copy(slot).start()
         w_wait(2, 0, (3,))
-        w_start(1, 2)
-        w_wait(1, 0, (3,))
         kept[2].wait()
         w_wait(2, 2)
         edge_copy(0).wait_recv()
         for slot in range(2):
             rows_copy(slot).wait_recv()
+        w_start(1, 2)
+        w_wait(1, 0, (3,))
+        convolve(0)
         w_wait(1, 2, (5,))
-        convolve(0)
         w_wait(1, 3, (6,))
         w_wait(2, 3)
         convolve(1)

time: 111 us -> 110 us (level)
  no operation moved by 1% of the time
where the time goes in v4:
time: 110 us
  Pallas kernels  108 us (98%)
  local copies, waits for them, and re-layouts  1.72 us (2%)
    pallas_call x1, Pallas kernels, block_call(): pl.pallas_call(functools.partial(block_kernel, shards, depth // HEADS), o...  108 us

profile of v4, /device:TPU:1, one launch (start us, length us, event | category | flops | bytes accessed | tf_op | source)
XLA Modules:
  0.0 109.5 jit_solution(8678362800491777529)
XLA Ops:
  0.0 107.8 %shard_map.91 = bf16[160,1024]{1,0:T(8,128)(2,1)} custom-call(s32[8]{0:T(128)} %bitcast.19, bf16[160,1024]{1,0:T(8,128)(2,1)} %bitcast.12, bf16[31,1024]{1,0:T(8,128)(2,1)} %bitcast.18, bf16[1024,128]{1,0:T(8,128)(2,1)} %bitcast.13, bf16[1024,128]{1,0:T(8,128)(2,1)} %bitcast.14, bf16[1024,128]{1,0:T(8,128)(2,1)} %bitcast.15, bf16[1024,128]{1,0:T(8,128)(2,1)} %bitcast.16, ...), custom_call_target="tpu_custom_call" | custom-call | tf_op jit(solution)/shard_map/pallas_call | solution.py:580
  107.8 1.7 %copy.11 = bf16[1,160,1024]{2,1,0:T(8,128)(2,1)} copy(bf16[1,160,1024]{2,1,0:T(8,128)(2,1)} %bitcast.10) | data formatting | bytes 655360

commit v5 on v4

--- a/solution.py
+++ b/solution.py
@@ -498,9 +498,9 @@
         w_wait(1, 0, (3,))
         convolve(0)
         w_wait(1, 2, (5,))
-        w_wait(1, 3, (6,))
         w_wait(2, 3)
         convolve(1)
+        w_wait(1, 3, (6,))
         for order in range(2):
             for at in range(0, part, 128):
                 deep_copy(order, at).wait_recv()

time: 110 us -> 106 us (0.964)
  Pallas kernels: 108 us -> 104 us
    pallas_call x1, Pallas kernels: 108 us -> 104 us  [block_call(): pl.pallas_call(functools.partial(block_kernel, shards, depth // HEADS), o...]
where the time goes in v5:
time: 106 us; the launch traced here: 105 us
  Pallas kernels  104 us (98%)
  local copies, waits for them, and re-layouts  1.72 us (2%)
    pallas_call x1, Pallas kernels, block_call(): pl.pallas_call(functools.partial(block_kernel, shards, depth // HEADS), o...  104 us

profile of v5, /device:TPU:1, one launch (start us, length us, event | category | flops | bytes accessed | tf_op | source)
XLA Modules:
  0.0 105.3 jit_solution(638148670864961338)
XLA Ops:
  0.0 103.5 %shard_map.91 = bf16[160,1024]{1,0:T(8,128)(2,1)} custom-call(s32[8]{0:T(128)} %bitcast.19, bf16[160,1024]{1,0:T(8,128)(2,1)} %bitcast.12, bf16[31,1024]{1,0:T(8,128)(2,1)} %bitcast.18, bf16[1024,128]{1,0:T(8,128)(2,1)} %bitcast.13, bf16[1024,128]{1,0:T(8,128)(2,1)} %bitcast.14, bf16[1024,128]{1,0:T(8,128)(2,1)} %bitcast.15, bf16[1024,128]{1,0:T(8,128)(2,1)} %bitcast.16, ...), custom_call_target="tpu_custom_call" | custom-call | tf_op jit(solution)/shard_map/pallas_call | solution.py:580
  103.6 1.7 %copy.11 = bf16[1,160,1024]{2,1,0:T(8,128)(2,1)} copy(bf16[1,160,1024]{2,1,0:T(8,128)(2,1)} %bitcast.10) | data formatting | bytes 655360
